TPU v7x, 32 devices: a whole 2x2x4 slice. The times are simulated.
32 devices in a mesh: cells: 32 (over z, y, x, core).
Axes of the slice: x: 2, y: 2, z: 4, core: 2. Of those that a mesh axis runs over, the one named last changes fastest.
Arguments:
- earlier_kinetics_concentrations: float32 [4096, 1536], P('cells'), may hold values from 0.05 to 1
- thermal_level: float32 [4096], P('cells'), may hold values from 0.8 to 2
- earlier_fluid_holder: int32 [4096], P('cells'), may hold values from 0 to 31, as said below
- earlier_fluid_slot: int32 [4096], P('cells'), may hold values from 0 to 127, as said below
- adjacent_volumes: int32 [6, 4096], P(None, 'cells'), may hold values from 0 to 4095, as said below
- interface_spreading_factor: float32 [6, 4096], P(None, 'cells'), may hold values from 0.2 to 1
- species_spreading_coefficient: float32 [1536], replicated, may hold values from 0.1 to 2
- present_kinetics_holder: int32 [4096], P('cells'), may hold values from 0 to 31, as said below
- present_kinetics_slot: int32 [4096], P('cells'), may hold values from 0 to 127, as said below
- natural_frequency_factor: float32 [4608], replicated, may hold values from -0.5 to 1
- arrhenius_energy: float32 [4608], replicated, may hold values from 0 to 2
- consumed_species: int32 [2, 4608], replicated, may hold values from 0 to 1535
- yielded_species: int32 [2, 4608], replicated, may hold values from 0 to 1535
Outputs:
- spread_concentration: float32 [4096, 1536], P('cells')
- chem_next: float32 [4096, 1536], P('cells')
Inputs may be any that keep to these rules, and one draw needn't show every extreme that they name: earlier_fluid_holder and earlier_fluid_slot together name every row of every flow owner exactly once; each device hands exactly 2 of its rows to each of 12 other devices and keeps the rest; each device receives exactly 2 rows from each of 12 devices. `earlier_fluid_slot`: rows of one flow owner. `adjacent_volumes`: each face names another cell at most 32 positions away in the flow order; on every device some face reaches exactly 32 away. present_kinetics_holder and present_kinetics_slot together name every row of every chemistry owner exactly once; each device hands exactly 2 of its cells to each of 12 other devices and keeps the rest; each device receives exactly 2 cells from each of 12 devices. `present_kinetics_slot`: rows of one chemistry owner.
All inputs are finite; a program needn't handle non-finite values.
Results may differ from a plain program's by a relative error of at most 0.0018.
Values sent between devices are 32-bit elements; how exact they have to be, the bound alone decides.
No kernel may reach another device: no remote copies, remote signals or barrier semaphores. Data moves between devices by JAX's collectives and lax.ppermute only.
A program may use at most 64 MiB of HBM per device.

v0:
```python
import math

import jax
import jax.numpy as jnp
from jax import lax
from jax.sharding import PartitionSpec as P

SPECIES = 1536
REACTIONS = 4608
NEWTON = 2
HALO = 32
CAP = 2


time_step = 0.5


def with_halo(value, sides, width):
    for axis, dim in sides:
        size, length = (lax.axis_size(axis), value.shape[dim])
        up = [(i, (i + 1) % size) for i in range(size - 1)]
        down = [(j, i) for i, j in up]
        last = lax.slice_in_dim(value, length - width, length, axis=dim)
        initial = lax.slice_in_dim(value, 0, width, axis=dim)
        before = lax.ppermute(last, axis, up)
        after = lax.ppermute(initial, axis, down)
        value = jnp.concatenate([before, value, after], axis=dim)
    return value


def bucket_rows(payload, owner, target_slot, owner_rank_index, partner_count):
    remote = owner != owner_rank_index
    choose = (
        (owner[:, None] == jnp.arange(partner_count, dtype=jnp.int32)[None, :]) & remote[:, None]
    ).astype(jnp.int32)
    earlier = jnp.cumsum(choose, axis=0) - choose
    within = jnp.sum(earlier * choose, axis=1)
    position = jnp.where(remote, owner * CAP + within, partner_count * CAP)
    packed = tuple(
        (
            jnp.zeros((partner_count * CAP,) + member.shape[1:], member.dtype)
            .at[position]
            .set(member, mode="drop")
            for member in payload
        )
    )
    slot_ids = (
        jnp.full((partner_count * CAP,), -1, jnp.int32).at[position].set(target_slot, mode="drop")
    )
    return (packed, slot_ids)


def assigned_lines(values, target_slot, keep, number_lines):
    index_rows = jnp.where(keep, target_slot, number_lines)
    return (
        jnp.zeros((number_lines,) + values.shape[1:], values.dtype)
        .at[index_rows]
        .set(values, mode="drop")
    )


def face_sum(extended, local_index, interface_spreading_factor):
    return jnp.sum(interface_spreading_factor[:, :, None] * extended[local_index], axis=0)


def newton_rates(
    initial, temper, natural_frequency_factor, arrhenius_energy, consumed_species, yielded_species
):
    reciprocal_mapping = 1.0 / temper
    block_width = math.gcd(REACTIONS, 512)
    species_rows = lax.broadcasted_iota(jnp.int32, (SPECIES, block_width), 0)

    def build_table(index_pair):
        return (species_rows == index_pair[0][None, :]).astype(jnp.bfloat16) + (
            species_rows == index_pair[1][None, :]
        ).astype(jnp.bfloat16)

    current = initial
    for newton_turn in range(NEWTON):
        log_state = jnp.log(current).astype(jnp.bfloat16)

        def add_block(block_index, partial_value):
            first_reaction = block_index * block_width
            react_table = build_table(
                lax.dynamic_slice_in_dim(consumed_species, first_reaction, block_width, 1)
            )
            product_table = build_table(
                lax.dynamic_slice_in_dim(yielded_species, first_reaction, block_width, 1)
            )
            log_rate = (
                lax.dynamic_slice_in_dim(natural_frequency_factor, first_reaction, block_width)[
                    None, :
                ]
                - lax.dynamic_slice_in_dim(arrhenius_energy, first_reaction, block_width)[None, :]
                * reciprocal_mapping[:, None]
            )
            exponent = jnp.dot(log_state, react_table, preferred_element_type=jnp.float32)
            rate_block = jnp.exp(log_rate + exponent).astype(jnp.bfloat16)
            loss_block = lax.dot_general(
                rate_block,
                react_table,
                (((1,), (1,)), ((), ())),
                preferred_element_type=jnp.float32,
            )
            gain_block = lax.dot_general(
                rate_block,
                product_table,
                (((1,), (1,)), ((), ())),
                preferred_element_type=jnp.float32,
            )
            return (partial_value[0] + loss_block, partial_value[1] + gain_block)

        zero_rows = jnp.zeros(current.shape, jnp.float32)
        loss_sum, gain_sum = lax.fori_loop(
            0, REACTIONS // block_width, add_block, (zero_rows, zero_rows)
        )
        current = (initial + time_step * gain_sum) / (1.0 + time_step * loss_sum / current)
    return current


def local(
    earlier_kinetics_concentrations,
    thermal_level,
    earlier_fluid_holder,
    earlier_fluid_slot,
    adjacent_volumes,
    interface_spreading_factor,
    species_spreading_coefficient,
    present_kinetics_holder,
    present_kinetics_slot,
    natural_frequency_factor,
    arrhenius_energy,
    consumed_species,
    yielded_species,
):
    owner_rank_index = lax.axis_index("cells")
    partner_count = lax.axis_size("cells")
    number_lines = earlier_kinetics_concentrations.shape[0]
    stays_onsite = earlier_fluid_holder == owner_rank_index
    flow_local = assigned_lines(
        earlier_kinetics_concentrations, earlier_fluid_slot, stays_onsite, number_lines
    )
    onsite_heat_level = assigned_lines(
        thermal_level, earlier_fluid_slot, stays_onsite, number_lines
    )
    local_index = adjacent_volumes - owner_rank_index * number_lines + HALO
    packed, slot_ids = bucket_rows(
        (earlier_kinetics_concentrations, thermal_level),
        earlier_fluid_holder,
        earlier_fluid_slot,
        owner_rank_index,
        partner_count,
    )
    moved_state, moved_temper, moved_slot = (
        lax.all_to_all(packed[0], "cells", split_axis=0, concat_axis=0, tiled=True),
        lax.all_to_all(packed[1], "cells", split_axis=0, concat_axis=0, tiled=True),
        lax.all_to_all(slot_ids, "cells", split_axis=0, concat_axis=0, tiled=True),
    )
    arrived = moved_slot >= 0
    flow_remote = assigned_lines(moved_state, moved_slot, arrived, number_lines)
    fluid_volume_heat = onsite_heat_level + assigned_lines(
        moved_temper, moved_slot, arrived, number_lines
    )
    flow_field = flow_local + flow_remote
    extended = with_halo(flow_field, (("cells", 0),), HALO)
    coupling = face_sum(extended, local_index, interface_spreading_factor)
    scale = time_step * species_spreading_coefficient[None, :]
    spread_concentration = (flow_field + scale * coupling) / (
        1.0 + scale * jnp.sum(interface_spreading_factor, axis=0)[:, None]
    )
    stays_home_mask = present_kinetics_holder == owner_rank_index
    packed_next, slot_next = bucket_rows(
        (spread_concentration, fluid_volume_heat),
        present_kinetics_holder,
        present_kinetics_slot,
        owner_rank_index,
        partner_count,
    )
    sent_state, sent_temper, sent_slot = (
        lax.all_to_all(packed_next[0], "cells", split_axis=0, concat_axis=0, tiled=True),
        lax.all_to_all(packed_next[1], "cells", split_axis=0, concat_axis=0, tiled=True),
        lax.all_to_all(slot_next, "cells", split_axis=0, concat_axis=0, tiled=True),
    )
    landed = sent_slot >= 0
    initial = assigned_lines(
        spread_concentration, present_kinetics_slot, stays_home_mask, number_lines
    ) + assigned_lines(sent_state, sent_slot, landed, number_lines)
    chem_temper = assigned_lines(
        fluid_volume_heat, present_kinetics_slot, stays_home_mask, number_lines
    ) + assigned_lines(sent_temper, sent_slot, landed, number_lines)
    chem_next = newton_rates(
        initial,
        chem_temper,
        natural_frequency_factor,
        arrhenius_energy,
        consumed_species,
        yielded_species,
    )
    return (spread_concentration, chem_next)


def solution(mesh):
    in_specs = (
        P("cells", None),
        P("cells"),
        P("cells"),
        P("cells"),
        P(None, "cells"),
        P(None, "cells"),
        P(),
        P("cells"),
        P("cells"),
        P(),
        P(),
        P(),
        P(),
    )
    out_specs = (P("cells", None), P("cells", None))
    return jax.shard_map(local, mesh=mesh, in_specs=in_specs, out_specs=out_specs, check_vma=False)
```

profile of v0, /device:TPU:0, one launch (start us, length us, event | category | flops | bytes accessed | tf_op | source)
XLA Modules:
  0.0 249.0 jit_solution(3540866650763344540)
XLA Ops:
  8.0 7.3 %all-to-all-start = ((s32[32,2,1]{1,2,0:T(1,128)}), s32[32,2,1]{1,2,0:T(1,128)S(1)}, u32[]{:S(2)}, u32[]{:S(2)}) async-start(s32[32,2,1]{1,2,0:T(1,128)} %bitcast), calls=%async_computation | async-start | bytes 32768 | tf_op jit(solution)/shard_map/all_to_all | solution.py:157
  18.1 4.3 %all-to-all-done = s32[32,2,1]{1,2,0:T(1,128)S(1)} async-done(((s32[32,2,1]{1,2,0:T(1,128)}), s32[32,2,1]{1,2,0:T(1,128)S(1)}, u32[]{:S(2)}, u32[]{:S(2)}) %all-to-all-start) | async-done | bytes 288 | tf_op jit(solution)/shard_map/all_to_all | solution.py:157
  22.4 2.6 %all-to-all-start.1 = ((f32[32,2,1536]{2,1,0:T(2,128)}), f32[32,2,1536]{2,1,0:T(2,128)S(1)}, u32[]{:S(2)}, u32[]{:S(2)}) async-start(f32[32,2,1536]{2,1,0:T(2,128)} %all_to_all.51), calls=%async_computation.1 | async-start | bytes 786432 | tf_op jit(solution)/shard_map/all_to_all | solution.py:155
  30.1 8.1 %all-to-all-done.1 = f32[32,2,1536]{2,1,0:T(2,128)S(1)} async-done(((f32[32,2,1536]{2,1,0:T(2,128)}), f32[32,2,1536]{2,1,0:T(2,128)S(1)}, u32[]{:S(2)}, u32[]{:S(2)}) %all-to-all-start.1) | async-done | bytes 393248 | tf_op jit(solution)/shard_map/all_to_all | solution.py:155
  38.2 2.5 %all-to-all-start.4 = ((f32[32,2,1]{1,2,0:T(1,128)}), f32[32,2,1]{1,2,0:T(1,128)S(1)}, u32[]{:S(2)}, u32[]{:S(2)}) async-start(f32[32,2,1]{1,2,0:T(1,128)} %bitcast.6), calls=%async_computation.4 | async-start | bytes 32768 | tf_op jit(solution)/shard_map/all_to_all | solution.py:156
  48.7 7.9 %all-to-all-start.2 = ((s32[32,2,1]{1,2,0:T(1,128)}), s32[32,2,1]{1,2,0:T(1,128)S(1)}, u32[]{:S(2)}, u32[]{:S(2)}) async-start(s32[32,2,1]{1,2,0:T(1,128)} %bitcast.4), calls=%async_computation.2 | async-start | bytes 32768 | tf_op jit(solution)/shard_map/all_to_all | solution.py:182
  60.6 4.1 %gather_fusion = f32[768,1536]{1,0:T(8,128)} fusion(f32[192,1536]{1,0:T(8,128)S(1)} %pad_maximum_fusion, s32[1024]{0:T(1024)S(1)} %pad_clamp_fusion), kind=kCustom, calls=%fused_computation | custom fusion | bytes 9440256 | tf_op jit(solution)/shard_map/gather | solution.py:63
  64.8 2.8 %multiply_reduce_fusion = f32[128,1536]{1,0:T(8,128)S(1)} fusion(f32[6,128,1536]{2,1,0:T(8,128)} %bitcast.77, f32[6,128]{1,0:T(8,128)S(1)} %copy-done.2), kind=kLoop, calls=%fused_computation.67 | loop fusion | flops 2162688 | bytes 5508096 | tf_op jit(solution)/shard_map/reduce_sum | solution.py:63
  67.6 5.8 %all-to-all-start.5 = ((f32[32,2,1]{1,2,0:T(1,128)}), f32[32,2,1]{1,2,0:T(1,128)S(1)}, u32[]{:S(2)}, u32[]{:S(2)}) async-start(f32[32,2,1]{1,2,0:T(1,128)} %bitcast.7), calls=%async_computation.5 | async-start | bytes 32768 | tf_op jit(solution)/shard_map/all_to_all | solution.py:181
  75.8 4.8 %all-to-all-done.5 = f32[32,2,1]{1,2,0:T(1,128)S(1)} async-done(((f32[32,2,1]{1,2,0:T(1,128)}), f32[32,2,1]{1,2,0:T(1,128)S(1)}, u32[]{:S(2)}, u32[]{:S(2)}) %all-to-all-start.5) | async-done | bytes 288 | tf_op jit(solution)/shard_map/all_to_all | solution.py:181
  80.6 2.6 %all-to-all-start.3 = ((f32[32,2,1536]{2,1,0:T(2,128)}), f32[32,2,1536]{2,1,0:T(2,128)S(1)}, u32[]{:S(2)}, u32[]{:S(2)}) async-start(f32[32,2,1536]{2,1,0:T(2,128)} %all_to_all.57), calls=%async_computation.3 | async-start | bytes 786432 | tf_op jit(solution)/shard_map/all_to_all | solution.py:180
  89.2 7.1 %all-to-all-done.3 = f32[32,2,1536]{2,1,0:T(2,128)S(1)} async-done(((f32[32,2,1536]{2,1,0:T(2,128)}), f32[32,2,1536]{2,1,0:T(2,128)S(1)}, u32[]{:S(2)}, u32[]{:S(2)}) %all-to-all-start.3) | async-done | bytes 393248 | tf_op jit(solution)/shard_map/all_to_all | solution.py:180
  99.7 68.5 %while.34 = (s32[]{:T(128)}, f32[128,1536]{1,0:T(8,128)S(1)}, f32[128,1536]{1,0:T(8,128)S(1)}, f32[4608]{0:T(1024)}, f32[4608]{0:T(1024)}, /*index=5*/f32[128]{0...) while((s32[]{:T(128)}, f32[128,1536]{1,0:T(8,128)S(1)}, ...), condition=%wide.region_21.22_spmd.clone.clone, body=%wide.region_20.21_spmd.clone.clone.sunk | while | flops 623902720 | bytes 4498166 | solution.py:114
  168.6 78.0 %while.35 = (s32[]{:T(128)}, f32[128,1536]{1,0:T(8,128)S(1)}, f32[128,1536]{1,0:T(8,128)}, f32[4608]{0:T(1024)}, f32[4608]{0:T(1024)}, /*index=5*/f32[128]{0:T(1...) while((s32[]{:T(128)}, f32[128,1536]{1,0:T(8,128)S(1)}, ...), condition=%wide.region_23.24_spmd.clone.clone, body=%wide.region_22.23_spmd.clone.clone.sunk | while | flops 623902720 | bytes 4498166 | solution.py:114
  173.2 2.8 %convolution_add_fusion.11 = f32[128,1536]{1,0:T(8,128)} fusion(bf16[128,512]{0,1:T(8,128)(2,1)} %fusion.131, s32[512]{0:T(512)S(1)} %bitcast.88, s32[512]{0:T(512)S(1)} %bitcast.89, f32[128,1536]{1,0:T(8,128)} %get-tuple-element.722, pred[]{:T(512)S(6)} %compare.7), kind=kOutput, calls=%fused_computation.50.clone.1 | convolution fusion | flops 208011264 | bytes 1708033 | tf_op jit(solution)/shard_map/while/body/eval_jaxpr/dot_general | solution.py:105
  181.7 3.0 %convolution_add_fusion.11 = f32[128,1536]{1,0:T(8,128)} fusion(bf16[128,512]{0,1:T(8,128)(2,1)} %fusion.131, s32[512]{0:T(512)S(1)} %bitcast.88, s32[512]{0:T(512)S(1)} %bitcast.89, f32[128,1536]{1,0:T(8,128)} %get-tuple-element.722, pred[]{:T(512)S(6)} %compare.7), kind=kOutput, calls=%fused_computation.50.clone.1 | convolution fusion | flops 208011264 | bytes 1708033 | tf_op jit(solution)/shard_map/while/body/eval_jaxpr/dot_general | solution.py:105
  190.4 3.0 %convolution_add_fusion.11 = f32[128,1536]{1,0:T(8,128)} fusion(bf16[128,512]{0,1:T(8,128)(2,1)} %fusion.131, s32[512]{0:T(512)S(1)} %bitcast.88, s32[512]{0:T(512)S(1)} %bitcast.89, f32[128,1536]{1,0:T(8,128)} %get-tuple-element.722, pred[]{:T(512)S(6)} %compare.7), kind=kOutput, calls=%fused_computation.50.clone.1 | convolution fusion | flops 208011264 | bytes 1708033 | tf_op jit(solution)/shard_map/while/body/eval_jaxpr/dot_general | solution.py:105
  199.1 3.0 %convolution_add_fusion.11 = f32[128,1536]{1,0:T(8,128)} fusion(bf16[128,512]{0,1:T(8,128)(2,1)} %fusion.131, s32[512]{0:T(512)S(1)} %bitcast.88, s32[512]{0:T(512)S(1)} %bitcast.89, f32[128,1536]{1,0:T(8,128)} %get-tuple-element.722, pred[]{:T(512)S(6)} %compare.7), kind=kOutput, calls=%fused_computation.50.clone.1 | convolution fusion | flops 208011264 | bytes 1708033 | tf_op jit(solution)/shard_map/while/body/eval_jaxpr/dot_general | solution.py:105
  207.8 3.0 %convolution_add_fusion.11 = f32[128,1536]{1,0:T(8,128)} fusion(bf16[128,512]{0,1:T(8,128)(2,1)} %fusion.131, s32[512]{0:T(512)S(1)} %bitcast.88, s32[512]{0:T(512)S(1)} %bitcast.89, f32[128,1536]{1,0:T(8,128)} %get-tuple-element.722, pred[]{:T(512)S(6)} %compare.7), kind=kOutput, calls=%fused_computation.50.clone.1 | convolution fusion | flops 208011264 | bytes 1708033 | tf_op jit(solution)/shard_map/while/body/eval_jaxpr/dot_general | solution.py:105
  216.4 3.0 %convolution_add_fusion.11 = f32[128,1536]{1,0:T(8,128)} fusion(bf16[128,512]{0,1:T(8,128)(2,1)} %fusion.131, s32[512]{0:T(512)S(1)} %bitcast.88, s32[512]{0:T(512)S(1)} %bitcast.89, f32[128,1536]{1,0:T(8,128)} %get-tuple-element.722, pred[]{:T(512)S(6)} %compare.7), kind=kOutput, calls=%fused_computation.50.clone.1 | convolution fusion | flops 208011264 | bytes 1708033 | tf_op jit(solution)/shard_map/while/body/eval_jaxpr/dot_general | solution.py:105
  225.1 3.0 %convolution_add_fusion.11 = f32[128,1536]{1,0:T(8,128)} fusion(bf16[128,512]{0,1:T(8,128)(2,1)} %fusion.131, s32[512]{0:T(512)S(1)} %bitcast.88, s32[512]{0:T(512)S(1)} %bitcast.89, f32[128,1536]{1,0:T(8,128)} %get-tuple-element.722, pred[]{:T(512)S(6)} %compare.7), kind=kOutput, calls=%fused_computation.50.clone.1 | convolution fusion | flops 208011264 | bytes 1708033 | tf_op jit(solution)/shard_map/while/body/eval_jaxpr/dot_general | solution.py:105
  233.8 3.0 %convolution_add_fusion.11 = f32[128,1536]{1,0:T(8,128)} fusion(bf16[128,512]{0,1:T(8,128)(2,1)} %fusion.131, s32[512]{0:T(512)S(1)} %bitcast.88, s32[512]{0:T(512)S(1)} %bitcast.89, f32[128,1536]{1,0:T(8,128)} %get-tuple-element.722, pred[]{:T(512)S(6)} %compare.7), kind=kOutput, calls=%fused_computation.50.clone.1 | convolution fusion | flops 208011264 | bytes 1708033 | tf_op jit(solution)/shard_map/while/body/eval_jaxpr/dot_general | solution.py:105
  242.5 3.0 %convolution_add_fusion.11 = f32[128,1536]{1,0:T(8,128)} fusion(bf16[128,512]{0,1:T(8,128)(2,1)} %fusion.131, s32[512]{0:T(512)S(1)} %bitcast.88, s32[512]{0:T(512)S(1)} %bitcast.89, f32[128,1536]{1,0:T(8,128)} %get-tuple-element.722, pred[]{:T(512)S(6)} %compare.7), kind=kOutput, calls=%fused_computation.50.clone.1 | convolution fusion | flops 208011264 | bytes 1708033 | tf_op jit(solution)/shard_map/while/body/eval_jaxpr/dot_general | solution.py:105
  246.6 2.4 add_divide_fusion
  (210 shorter events, 157.6 us)
Async XLA Ops:
  0.6 28.1 %copy-start.3 = (f32[1536]{0:T(1024)S(1)}, f32[1536]{0:T(1024)}, u32[]{:S(2)}) copy-start(f32[1536]{0:T(1024)} %param.23) | copy-start | bytes 18436
  8.0 14.4 %all-to-all-start = ((s32[32,2,1]{1,2,0:T(1,128)}), s32[32,2,1]{1,2,0:T(1,128)S(1)}, u32[]{:S(2)}, u32[]{:S(2)}) async-start(s32[32,2,1]{1,2,0:T(1,128)} %bitcast), calls=%async_computation | async-start | bytes 32768 | tf_op jit(solution)/shard_map/all_to_all | solution.py:157
  18.1 27.6 %copy-start.4 = (s32[6,128]{1,0:T(8,128)S(1)}, s32[6,128]{1,0:T(8,128)}, u32[]{:S(2)}) copy-start(s32[6,128]{1,0:T(8,128)} %param.21) | copy-start | bytes 9220
  18.1 28.7 %copy-start.2 = (f32[6,128]{1,0:T(8,128)S(1)}, f32[6,128]{1,0:T(8,128)}, u32[]{:S(2)}) copy-start(f32[6,128]{1,0:T(8,128)} %param.22) | copy-start | bytes 9220
  22.4 15.8 %all-to-all-start.1 = ((f32[32,2,1536]{2,1,0:T(2,128)}), f32[32,2,1536]{2,1,0:T(2,128)S(1)}, u32[]{:S(2)}, u32[]{:S(2)}) async-start(f32[32,2,1536]{2,1,0:T(2,128)} %all_to_all.51), calls=%async_computation.1 | async-start | bytes 786432 | tf_op jit(solution)/shard_map/all_to_all | solution.py:155
  38.2 10.5 %all-to-all-start.4 = ((f32[32,2,1]{1,2,0:T(1,128)}), f32[32,2,1]{1,2,0:T(1,128)S(1)}, u32[]{:S(2)}, u32[]{:S(2)}) async-start(f32[32,2,1]{1,2,0:T(1,128)} %bitcast.6), calls=%async_computation.4 | async-start | bytes 32768 | tf_op jit(solution)/shard_map/all_to_all | solution.py:156
  42.2 18.3 %collective-permute-start = (f32[32,1536]{1,0:T(8,128)S(1)}, f32[32,1536]{1,0:T(8,128)S(1)}, u32[]{:S(2)}, u32[]{:S(2)}) collective-permute-start(f32[32,1536]{1,0:T(8,128)S(1)} %get-tuple-element.530), channel_id=1, source_target_pairs={{0,1},{1,2},{2,3},{3,4},{4,5},{5,6},{6,7},{7,8},{8,9},{9,10},{10,1... | collective-permute-start | bytes 589832 | tf_op jit(solution)/shard_map/ppermute | solution.py:25
  44.4 16.2 %collective-permute-start.1 = (f32[32,1536]{1,0:T(8,128)S(1)}, f32[32,1536]{1,0:T(8,128)S(1)}, u32[]{:S(2)}, u32[]{:S(2)}) collective-permute-start(f32[32,1536]{1,0:T(8,128)S(1)} %get-tuple-element.531), channel_id=1, source_target_pairs={{1,0},{2,1},{3,2},{4,3},{5,4},{6,5},{7,6},{8,7},{9,8},{10,9},{11,1... | collective-permute-start | bytes 589832 | tf_op jit(solution)/shard_map/ppermute | solution.py:26
  48.7 18.9 %all-to-all-start.2 = ((s32[32,2,1]{1,2,0:T(1,128)}), s32[32,2,1]{1,2,0:T(1,128)S(1)}, u32[]{:S(2)}, u32[]{:S(2)}) async-start(s32[32,2,1]{1,2,0:T(1,128)} %bitcast.4), calls=%async_computation.2 | async-start | bytes 32768 | tf_op jit(solution)/shard_map/all_to_all | solution.py:182
  67.6 13.0 %all-to-all-start.5 = ((f32[32,2,1]{1,2,0:T(1,128)}), f32[32,2,1]{1,2,0:T(1,128)S(1)}, u32[]{:S(2)}, u32[]{:S(2)}) async-start(f32[32,2,1]{1,2,0:T(1,128)} %bitcast.7), calls=%async_computation.5 | async-start | bytes 32768 | tf_op jit(solution)/shard_map/all_to_all | solution.py:181
  73.6 6.9 %copy-start.1 = (f32[128,1536]{1,0:T(8,128)}, f32[128,1536]{1,0:T(8,128)S(1)}, u32[]{:S(2)}) copy-start(f32[128,1536]{1,0:T(8,128)S(1)} %add_divide_fusion.1) | copy-start | bytes 2359300
  80.6 15.8 %all-to-all-start.3 = ((f32[32,2,1536]{2,1,0:T(2,128)}), f32[32,2,1536]{2,1,0:T(2,128)S(1)}, u32[]{:S(2)}, u32[]{:S(2)}) async-start(f32[32,2,1536]{2,1,0:T(2,128)} %all_to_all.57), calls=%async_computation.3 | async-start | bytes 786432 | tf_op jit(solution)/shard_map/all_to_all | solution.py:180
  99.7 68.9 %copy-start = (f32[128,1536]{1,0:T(8,128)S(1)}, f32[128,1536]{1,0:T(8,128)}, u32[]{:S(2)}) copy-start(f32[128,1536]{1,0:T(8,128)} %custom-call.2) | copy-start | bytes 2359300
  112.0 2.0 copy-start.5
  119.6 2.0 copy-start.5
  173.2 2.8 %copy-start.6 = (bf16[128,512]{0,1:T(8,128)(2,1)S(1)}, bf16[128,512]{0,1:T(8,128)(2,1)}, u32[]{:S(2)}) copy-start(bf16[128,512]{0,1:T(8,128)(2,1)} %fusion.131) | copy-start | bytes 393220 | tf_op jit(solution)/shard_map/while
  181.7 3.1 %copy-start.6 = (bf16[128,512]{0,1:T(8,128)(2,1)S(1)}, bf16[128,512]{0,1:T(8,128)(2,1)}, u32[]{:S(2)}) copy-start(bf16[128,512]{0,1:T(8,128)(2,1)} %fusion.131) | copy-start | bytes 393220 | tf_op jit(solution)/shard_map/while
  190.4 3.1 %copy-start.6 = (bf16[128,512]{0,1:T(8,128)(2,1)S(1)}, bf16[128,512]{0,1:T(8,128)(2,1)}, u32[]{:S(2)}) copy-start(bf16[128,512]{0,1:T(8,128)(2,1)} %fusion.131) | copy-start | bytes 393220 | tf_op jit(solution)/shard_map/while
  199.1 3.1 %copy-start.6 = (bf16[128,512]{0,1:T(8,128)(2,1)S(1)}, bf16[128,512]{0,1:T(8,128)(2,1)}, u32[]{:S(2)}) copy-start(bf16[128,512]{0,1:T(8,128)(2,1)} %fusion.131) | copy-start | bytes 393220 | tf_op jit(solution)/shard_map/while
  207.8 3.1 %copy-start.6 = (bf16[128,512]{0,1:T(8,128)(2,1)S(1)}, bf16[128,512]{0,1:T(8,128)(2,1)}, u32[]{:S(2)}) copy-start(bf16[128,512]{0,1:T(8,128)(2,1)} %fusion.131) | copy-start | bytes 393220 | tf_op jit(solution)/shard_map/while
  216.4 3.1 %copy-start.6 = (bf16[128,512]{0,1:T(8,128)(2,1)S(1)}, bf16[128,512]{0,1:T(8,128)(2,1)}, u32[]{:S(2)}) copy-start(bf16[128,512]{0,1:T(8,128)(2,1)} %fusion.131) | copy-start | bytes 393220 | tf_op jit(solution)/shard_map/while
  225.1 3.1 %copy-start.6 = (bf16[128,512]{0,1:T(8,128)(2,1)S(1)}, bf16[128,512]{0,1:T(8,128)(2,1)}, u32[]{:S(2)}) copy-start(bf16[128,512]{0,1:T(8,128)(2,1)} %fusion.131) | copy-start | bytes 393220 | tf_op jit(solution)/shard_map/while
  233.8 3.1 %copy-start.6 = (bf16[128,512]{0,1:T(8,128)(2,1)S(1)}, bf16[128,512]{0,1:T(8,128)(2,1)}, u32[]{:S(2)}) copy-start(bf16[128,512]{0,1:T(8,128)(2,1)} %fusion.131) | copy-start | bytes 393220 | tf_op jit(solution)/shard_map/while
  242.5 3.1 %copy-start.6 = (bf16[128,512]{0,1:T(8,128)(2,1)S(1)}, bf16[128,512]{0,1:T(8,128)(2,1)}, u32[]{:S(2)}) copy-start(bf16[128,512]{0,1:T(8,128)(2,1)} %fusion.131) | copy-start | bytes 393220 | tf_op jit(solution)/shard_map/while
  (7 other events, 13.8 us)
where the time goes:
time: 252 us; the launch traced here: 249 us
  matrix products  103 us (41%)
  local copies, waits for them, and re-layouts  71.5 us (28%)
  starting transfers between devices  32.3 us (13%)
  waiting for transfers between devices  24.3 us (10%)
  other arithmetic  16.2 us (6%)
    dot_general x18, matrix products, add_block(): lax.dot_general(rate_block, product_table, (((1,), (1,)), ((), ())), pref...  44.8 us
    dot_general x18, matrix products, add_block(): jnp.dot(log_state, react_table, preferred_element_type=jnp.float32)  40.3 us
    dot_general x18, matrix products, add_block(): lax.dot_general(rate_block, react_table, (((1,), (1,)), ((), ())), prefer...  17.9 us
    slice x18, local copies, waits for them, and re-layouts, build_table(): index_pair[0][None, :]  15.3 us
    dynamic_slice x18, local copies, waits for them, and re-layouts, add_block(): lax.dynamic_slice_in_dim(arrhenius_energy, first_reaction, block_width)  13.7 us
    dynamic_slice x18, local copies, waits for them, and re-layouts, add_block(): lax.dynamic_slice_in_dim(natural_frequency_factor, first_reaction, block_...  13.7 us
    scatter x8, local copies, waits for them, and re-layouts, assigned_lines(): return jnp.zeros((number_lines,) + values.shape[1:], values.dtype).at[ind...  10.4 us
    all_to_all x1, waiting for transfers between devices, local(): lax.all_to_all(packed[0], 'cells', split_axis=0, concat_axis=0, tiled=True)  8.07 us
  transfers between devices with their start and end apart: 8, of which 4 were waited for; matrix products, arithmetic and copies ran while one was open for 11% of the time, Pallas kernels for 0%

commit v1 on v0

v1 whole, which is shorter than its diff:
```python
import functools

import jax
import jax.numpy as jnp
from jax import lax
from jax.experimental import pallas as pl
from jax.experimental.pallas import tpu as pltpu
from jax.sharding import PartitionSpec as P

NEWTON = 2
HALO = 32
CAP = 2
EXTRA = 128

time_step = 0.5

f32 = jnp.float32
bf16 = jnp.bfloat16
i32 = jnp.int32
i16 = jnp.int16

VMEM = pl.BlockSpec(memory_space=pltpu.VMEM)
SMEM = pl.BlockSpec(memory_space=pltpu.SMEM)


def iota(shape, dim):
    return lax.broadcasted_iota(i32, shape, dim)


def column(row):
    n = row.shape[1]
    eye = iota((n, n), 0) == iota((n, n), 1)
    return jnp.sum(jnp.where(eye, row, jnp.zeros_like(row)), axis=1, keepdims=True)


def split3(x):
    hi = x.astype(bf16)
    rest = x - hi.astype(f32)
    mid = rest.astype(bf16)
    lo = (rest - mid.astype(f32)).astype(bf16)
    return hi, mid, lo


def pick(choice, rows, dims=(((1,), (0,)), ((), ()))):
    choice = choice.astype(bf16)
    out = None
    for part in split3(rows):
        term = lax.dot_general(choice, part, dims, preferred_element_type=f32)
        out = term if out is None else out + term
    return out


def send_choice(owner, me, partners):
    n = owner.shape[1]
    hits = ((iota((partners, n), 0) == owner) & (owner != me)).astype(f32)
    before = (iota((n, n), 0) < iota((n, n), 1)).astype(bf16)
    earlier = jnp.dot(hits.astype(bf16), before, preferred_element_type=f32)
    within = jnp.sum(earlier * hits, axis=0, keepdims=True).astype(i32)
    position = jnp.where(owner != me, owner * CAP + within, -1)
    return (iota((partners * CAP, n), 0) == position).astype(f32)


def pack(send_ref, rows, temper, owner, slot, me):
    partners, cap, _ = send_ref.shape
    n, species = rows.shape
    lane = iota((n, EXTRA), 1)
    beside = jnp.where(
        lane == 0, temper, jnp.where(lane == 1, column(slot.astype(f32)) + 1.0, 0.0)
    )
    choice = send_choice(owner, me, partners)
    send_ref[:, :, :species] = pick(choice, rows).reshape(partners, cap, species)
    send_ref[:, :, species:] = pick(choice, beside).reshape(partners, cap, EXTRA)


def unpack(recv_ref, rows, temper, owner, slot, me):
    partners, cap, width = recv_ref.shape
    n, species = rows.shape
    stay = ((iota((n, n), 0) == slot) & (owner == me)).astype(f32)
    got = recv_ref[...].reshape(partners * cap, width)
    place = got[:, species + 1 : species + 2].astype(i32) - 1
    land = (iota((partners * cap, n), 1) == place).astype(f32)
    to_rows = (((0,), (0,)), ((), ()))
    beside = jnp.broadcast_to(temper, (n, EXTRA))
    state = pick(stay, rows) + pick(land, got[:, :species], to_rows)
    heat = pick(stay, beside) + pick(land, got[:, species:], to_rows)
    return state, heat[:, 0:1]


def pack_kernel(me_ref, rows_ref, temper_ref, owner_ref, slot_ref, send_ref):
    pack(
        send_ref,
        rows_ref[...],
        column(temper_ref[...]),
        owner_ref[...],
        slot_ref[...],
        me_ref[0],
    )


def flow_kernel(
    me_ref, recv_ref, rows_ref, temper_ref, owner_ref, slot_ref, flow_ref, heat_ref, up_ref, down_ref
):
    state, heat = unpack(
        recv_ref,
        rows_ref[...],
        column(temper_ref[...]),
        owner_ref[...],
        slot_ref[...],
        me_ref[0],
    )
    n = state.shape[0]
    flow_ref[...] = state
    heat_ref[...] = jnp.broadcast_to(heat, heat_ref.shape)
    up_ref[...] = state[n - HALO :]
    down_ref[...] = state[:HALO]


def spread_kernel(
    me_ref,
    flow_ref,
    heat_ref,
    before_ref,
    after_ref,
    adjacent_ref,
    factor_ref,
    coefficient_ref,
    owner_ref,
    slot_ref,
    spread_ref,
    send_ref,
):
    me = me_ref[0]
    flow = flow_ref[...]
    n = flow.shape[0]
    faces = adjacent_ref.shape[0]
    index = adjacent_ref[...] - me * n + HALO
    factor = factor_ref[...]
    rows = iota((n + 2 * HALO, n), 0)
    weight = jnp.zeros((n + 2 * HALO, n), f32)
    total = jnp.zeros((1, n), f32)
    for face in range(faces):
        weight += jnp.where(rows == index[face : face + 1], factor[face : face + 1], 0.0)
        total += factor[face : face + 1]
    extended = jnp.concatenate([before_ref[...], flow, after_ref[...]], axis=0)
    w_hi, w_mid, _ = split3(weight)
    e_hi, e_mid, _ = split3(extended)
    dims = (((0,), (0,)), ((), ()))
    coupling = (
        lax.dot_general(w_hi, e_hi, dims, preferred_element_type=f32)
        + lax.dot_general(w_hi, e_mid, dims, preferred_element_type=f32)
        + lax.dot_general(w_mid, e_hi, dims, preferred_element_type=f32)
    )
    scale = time_step * coefficient_ref[...]
    spread = (flow + scale * coupling) / (1.0 + scale * column(total))
    spread_ref[...] = spread
    pack(send_ref, spread, heat_ref[:, 0:1], owner_ref[...], slot_ref[...], me)


def table(index_iota, first, second):
    one, zero = jnp.ones((), bf16), jnp.zeros((), bf16)
    return jnp.where(index_iota == first, one, zero) + jnp.where(index_iota == second, one, zero)


def newton_kernel(
    me_ref,
    recv_ref,
    spread_ref,
    heat_ref,
    owner_ref,
    slot_ref,
    frequency_ref,
    energy_ref,
    species_ref,
    out_ref,
    react_ref,
    react_t_ref,
    product_t_ref,
    initial_ref,
    loss_ref,
    gain_ref,
    log_ref,
):
    initial, heat = unpack(
        recv_ref,
        spread_ref[...],
        heat_ref[:, 0:1],
        owner_ref[...],
        slot_ref[...],
        me_ref[0],
    )
    inverse = 1.0 / heat
    initial_ref[...] = initial
    out_ref[...] = initial
    species = initial.shape[1]
    reactions = frequency_ref.shape[1]

    for turn in range(NEWTON):
        wanted = (512, 256, 128) if turn == 0 else (1536, 768, 512, 256, 128)
        block = next(b for b in wanted if reactions % b == 0)
        log_ref[...] = jnp.log(out_ref[...]).astype(bf16)
        loss_ref[...] = jnp.zeros_like(loss_ref)
        gain_ref[...] = jnp.zeros_like(gain_ref)
        if turn == 0:
            down_species = iota((species, block), 0).astype(i16)
            along_species = iota((block, species), 1).astype(i16)

        def add_block(b, carry):
            at = pl.ds(pl.multiple_of(b * block, block), block)
            if turn == 0:
                index = species_ref[:, at]
                columns = jnp.transpose(index).astype(i16)
                react_ref[:, at] = table(
                    down_species, index[0:1].astype(i16), index[1:2].astype(i16)
                )
                react_t_ref[at, :] = table(along_species, columns[:, 0:1], columns[:, 1:2])
                product_t_ref[at, :] = table(along_species, columns[:, 2:3], columns[:, 3:4])
            exponent = jnp.dot(log_ref[...], react_ref[:, at], preferred_element_type=f32)
            log_rate = frequency_ref[:, at] - energy_ref[:, at] * inverse
            rate = jnp.exp(log_rate + exponent).astype(bf16)
            loss_ref[...] += jnp.dot(rate, react_t_ref[at, :], preferred_element_type=f32)
            gain_ref[...] += jnp.dot(rate, product_t_ref[at, :], preferred_element_type=f32)
            return carry

        lax.fori_loop(0, reactions // block, add_block, 0)
        out_ref[...] = (initial_ref[...] + time_step * gain_ref[...]) / (
            1.0 + time_step * loss_ref[...] / out_ref[...]
        )


def call(kernel, inputs, outputs, scratch=(), limit=32):
    return pl.pallas_call(
        kernel,
        out_shape=tuple(jax.ShapeDtypeStruct(shape, f32) for shape in outputs),
        in_specs=[SMEM] + [VMEM] * (len(inputs) - 1),
        out_specs=tuple([VMEM] * len(outputs)),
        scratch_shapes=list(scratch),
        compiler_params=pltpu.CompilerParams(vmem_limit_bytes=limit * 2**20),
    )(*inputs)


def local(
    earlier_kinetics_concentrations,
    thermal_level,
    earlier_fluid_holder,
    earlier_fluid_slot,
    adjacent_volumes,
    interface_spreading_factor,
    species_spreading_coefficient,
    present_kinetics_holder,
    present_kinetics_slot,
    natural_frequency_factor,
    arrhenius_energy,
    consumed_species,
    yielded_species,
):
    n, species = earlier_kinetics_concentrations.shape
    reactions = natural_frequency_factor.shape[0]
    partners = lax.axis_size("cells")
    me = lax.axis_index("cells").astype(i32).reshape(1)
    row = lambda x: x.reshape(1, -1)
    temper, owner, slot = row(thermal_level), row(earlier_fluid_holder), row(earlier_fluid_slot)
    next_owner, next_slot = row(present_kinetics_holder), row(present_kinetics_slot)
    buffer = (partners, CAP, species + EXTRA)

    def exchange(x):
        return lax.all_to_all(x, "cells", split_axis=0, concat_axis=0, tiled=True)

    (send,) = call(
        pack_kernel, (me, earlier_kinetics_concentrations, temper, owner, slot), (buffer,)
    )
    flow, heat, last, first = call(
        flow_kernel,
        (me, exchange(send), earlier_kinetics_concentrations, temper, owner, slot),
        ((n, species), (n, EXTRA), (HALO, species), (HALO, species)),
    )
    up = [(i, i + 1) for i in range(partners - 1)]
    down = [(i + 1, i) for i in range(partners - 1)]
    before = lax.ppermute(last, "cells", up)
    after = lax.ppermute(first, "cells", down)
    spread, send = call(
        spread_kernel,
        (
            me,
            flow,
            heat,
            before,
            after,
            adjacent_volumes,
            interface_spreading_factor,
            row(species_spreading_coefficient),
            next_owner,
            next_slot,
        ),
        ((n, species), buffer),
    )
    index = jnp.concatenate(
        [consumed_species, yielded_species, jnp.zeros((4, reactions), i32)], axis=0
    )
    (chem_next,) = call(
        newton_kernel,
        (
            me,
            exchange(send),
            spread,
            heat,
            next_owner,
            next_slot,
            row(natural_frequency_factor),
            row(arrhenius_energy),
            index,
        ),
        ((n, species),),
        scratch=(
            pltpu.VMEM((species, reactions), bf16),
            pltpu.VMEM((reactions, species), bf16),
            pltpu.VMEM((reactions, species), bf16),
            pltpu.VMEM((n, species), f32),
            pltpu.VMEM((n, species), f32),
            pltpu.VMEM((n, species), f32),
            pltpu.VMEM((n, species), bf16),
        ),
        limit=62,
    )
    return (spread, chem_next)


def solution(mesh):
    in_specs = (
        P("cells", None),
        P("cells"),
        P("cells"),
        P("cells"),
        P(None, "cells"),
        P(None, "cells"),
        P(),
        P("cells"),
        P("cells"),
        P(),
        P(),
        P(),
        P(),
    )
    out_specs = (P("cells", None), P("cells", None))
    return jax.shard_map(local, mesh=mesh, in_specs=in_specs, out_specs=out_specs, check_vma=False)
```

time: 252 us -> 81 us (0.32)
  matrix products: 103 us -> 0 us
  local copies, waits for them, and re-layouts: 71.5 us -> 4.59 us
  Pallas kernels: 0 us -> 27.6 us
  blocking collectives: 0 us -> 20.9 us
  starting transfers between devices: 32.3 us -> 11.8 us
  other arithmetic: 16.2 us -> 0.73 us
  waiting for transfers between devices: 24.3 us -> 14.1 us
    dot_general x54 -> x0, matrix products: 103 us -> none  [the longest x18 44.8 us: add_block(): lax.dot_general(rate_block, product_table, (((1,), (1,)), ((), ())), pref...]
    pallas_call x0 -> x4, Pallas kernels: none -> 27.6 us  [call(): pl.pallas_call(kernel, out_shape=tuple((jax.ShapeDtypeStruct(shape, f32)...]
    dynamic_slice x36 -> x0, local copies, waits for them, and re-layouts: 27.4 us -> none  [the longest x18 13.7 us: add_block(): lax.dynamic_slice_in_dim(arrhenius_energy, first_reaction, block_width)]
    all_to_all x0 -> x1, blocking collectives: none -> 20.9 us  [exchange(): return lax.all_to_all(x, 'cells', split_axis=0, concat_axis=0, tiled=True)]
    all_to_all x6 -> x1, starting transfers between devices: 28.8 us -> 8.77 us  [exchange(): return lax.all_to_all(x, 'cells', split_axis=0, concat_axis=0, tiled=True)]
    scatter x14 -> x0, local copies, waits for them, and re-layouts: 17.7 us -> none  [the longest x8 10.4 us: assigned_lines(): return jnp.zeros((number_lines,) + values.shape[1:], values.dtype).at[ind...]
    slice x19 -> x0, local copies, waits for them, and re-layouts: 15.4 us -> none  [the longest x18 15.3 us: build_table(): index_pair[0][None, :]]
    all_to_all x6 -> x1, waiting for transfers between devices: 24.3 us -> 13 us  [exchange(): return lax.all_to_all(x, 'cells', split_axis=0, concat_axis=0, tiled=True)]
  transfers between devices with their start and end apart: 8 -> 3, of which waited for: 4 -> 2; matrix products, arithmetic and copies ran while one was open for 11% -> 3% of each run, Pallas kernels for 0% -> 0%
where the time goes in v1:
time: 81 us; the launch traced here: 80.5 us
  Pallas kernels  27.6 us (34%)
  blocking collectives  20.9 us (26%)
  waiting for transfers between devices  14.1 us (17%)
  starting transfers between devices  11.8 us (15%)
  local copies, waits for them, and re-layouts  4.59 us (6%)
    pallas_call x4, Pallas kernels, call(): pl.pallas_call(kernel, out_shape=tuple((jax.ShapeDtypeStruct(shape, f32)...  27.6 us
    all_to_all x1, blocking collectives, exchange(): return lax.all_to_all(x, 'cells', split_axis=0, concat_axis=0, tiled=True)  20.9 us
    all_to_all x1, waiting for transfers between devices, exchange(): return lax.all_to_all(x, 'cells', split_axis=0, concat_axis=0, tiled=True)  13 us
    all_to_all x1, starting transfers between devices, exchange(): return lax.all_to_all(x, 'cells', split_axis=0, concat_axis=0, tiled=True)  8.77 us
    unnamed x30, local copies, waits for them, and re-layouts  3.28 us
    ppermute x1, starting transfers between devices, local(): before = lax.ppermute(last, 'cells', up)  1.77 us
  transfers between devices with their start and end apart: 3, of which 2 were waited for; matrix products, arithmetic and copies ran while one was open for 3% of the time, Pallas kernels for 0%

profile of v1, /device:TPU:0, one launch (start us, length us, event | category | flops | bytes accessed | tf_op | source)
XLA Modules:
  0.0 80.5 jit_solution(3633076831611483885)
XLA Ops:
  0.7 0.6 copy-done.4
  1.3 0.0 copy-done.5
  1.3 0.0 copy-done.6
  1.3 1.1 %copy-done = f32[128,1536]{1,0:T(8,128)S(1)} copy-done((f32[128,1536]{1,0:T(8,128)S(1)}, f32[128,1536]{1,0:T(8,128)}, u32[]{:S(2)}) %copy-start) | copy-done | bytes 786456
  2.5 0.5 shard_map.140
  3.0 20.9 %all_to_all.10.recv_ref = f32[32,2,1664]{2,1,0:T(2,128)S(1)} all-to-all(f32[32,2,1664]{2,1,0:T(2,128)S(1)} %shard_map.140), channel_id=1, replica_groups=mesh['cells'=32] {'cells'}, dimensions={0} | all-to-all | bytes 851968 | tf_op jit(solution)/shard_map/all_to_all | solution.py:266
  23.8 1.0 %shard_map.141 = (f32[128,1536]{1,0:T(8,128)S(1)}, f32[128,128]{1,0:T(8,128)S(1)}, f32[32,1536]{1,0:T(8,128)S(1)}, f32[32,1536]{1,0:T(8,128)S(1)}) custom-call(s32[1]{0:T(128)} %bitcast.me_ref, f32[32,2,1664]{2,1,0:T(2,128)S(1)} %all_to_all.10.recv_ref, f32[128,1536]{1,0:T(8,128)S(1)} %copy-done, f32[1,128]{1,0:T(1,128)S(1)} %bitcast.7, ...), custom_call_target="tpu_custom_call" | custom-call | tf_op jit(solution)/shard_map/pallas_call | solution.py:231
  24.9 0.0 copy-start.12
  24.9 1.8 %collective-permute-start = (f32[32,1536]{1,0:T(8,128)S(1)}, f32[32,1536]{1,0:T(8,128)S(1)}, u32[]{:S(2)}, u32[]{:S(2)}) collective-permute-start(f32[32,1536]{1,0:T(8,128)S(1)} %get-tuple-element.10), channel_id=1, source_target_pairs={{0,1},{1,2},{2,3},{3,4},{4,5},{5,6},{6,7},{7,8},{8,9},{9,10},{10,1... | collective-permute-start | bytes 589832 | tf_op jit(solution)/shard_map/ppermute | solution.py:278
  26.7 1.3 %collective-permute-start.1 = (f32[32,1536]{1,0:T(8,128)S(1)}, f32[32,1536]{1,0:T(8,128)S(1)}, u32[]{:S(2)}, u32[]{:S(2)}) collective-permute-start(f32[32,1536]{1,0:T(8,128)S(1)} %get-tuple-element.11), channel_id=1, source_target_pairs={{1,0},{2,1},{3,2},{4,3},{5,4},{6,5},{7,6},{8,7},{9,8},{10,9},{11,1... | collective-permute-start | bytes 589832 | tf_op jit(solution)/shard_map/ppermute | solution.py:279
  28.0 0.0 copy-start.13
  28.0 0.1 pad.2.clone
  28.1 0.6 reshape.38.frequency_ref
  28.7 0.0 copy-done.13
  28.7 0.6 reshape.39.energy_ref
  29.3 1.1 %collective-permute-done.1.after_ref = f32[32,1536]{1,0:T(8,128)S(1)} collective-permute-done((f32[32,1536]{1,0:T(8,128)S(1)}, f32[32,1536]{1,0:T(8,128)S(1)}, u32[]{:S(2)}, u32[]{:S(2)}) %collective-permute-start.1) | collective-permute-done | bytes 196640 | tf_op jit(solution)/shard_map/ppermute | solution.py:279
  30.5 0.6 copy-done.7
  31.1 0.0 copy-done.8
  31.1 1.8 %shard_map.142 = (f32[128,1536]{1,0:T(8,128)}, f32[32,2,1664]{2,1,0:T(2,128)}) custom-call(s32[1]{0:T(128)} %bitcast.me_ref, f32[128,1536]{1,0:T(8,128)S(1)} %get-tuple-element.8.flow_ref, f32[128,128]{1,0:T(8,128)S(1)} %get-tuple-element.9.heat_ref, f32[32,1536]{1,0:T(8,128)S(1)} %collective-permute-done.before_ref, ...), custom_call_target="tpu_custom_call" | custom-call | tf_op jit(solution)/shard_map/pallas_call | solution.py:231
  32.9 8.8 %all-to-all-start.1 = ((f32[32,2,1664]{2,1,0:T(2,128)}), f32[32,2,1664]{2,1,0:T(2,128)S(1)}, u32[]{:S(2)}, u32[]{:S(2)}) async-start(f32[32,2,1664]{2,1,0:T(2,128)} %get-tuple-element.13), calls=%async_computation.1 | async-start | bytes 851968 | tf_op jit(solution)/shard_map/all_to_all | solution.py:266
  41.7 0.7 add_add_fusion.species_ref
  42.4 13.0 %all-to-all-done.1.recv_ref = f32[32,2,1664]{2,1,0:T(2,128)S(1)} async-done(((f32[32,2,1664]{2,1,0:T(2,128)}), f32[32,2,1664]{2,1,0:T(2,128)S(1)}, u32[]{:S(2)}, u32[]{:S(2)}) %all-to-all-start.1) | async-done | bytes 426016 | tf_op jit(solution)/shard_map/all_to_all | solution.py:266
  55.4 0.8 copy-done.9
  56.2 24.3 %shard_map.143 = f32[128,1536]{1,0:T(8,128)} custom-call(s32[1]{0:T(128)} %bitcast.me_ref, f32[32,2,1664]{2,1,0:T(2,128)} %copy-done.9, f32[128,1536]{1,0:T(8,128)} %get-tuple-element.6.spread_ref, f32[128,128]{1,0:T(8,128)} %copy-done.1, s32[1,128]{1,0:T(1,128)} %bitcast.12, s32[1,128]{1,0:T(1,128)} %bitcast.14, f32[1,4608]{1,0:T(1,128)} %reshape.38.frequency_ref, ...), custom_call_target="tpu_custom_call" | custom-call | tf_op jit(solution)/shard_map/pallas_call | solution.py:231
  (23 shorter events, 0.0 us)
Async XLA Ops:
  0.6 0.7 copy-start.4
  0.6 0.7 copy-start.5
  0.7 0.7 copy-start.6
  1.3 1.1 %copy-start = (f32[128,1536]{1,0:T(8,128)S(1)}, f32[128,1536]{1,0:T(8,128)}, u32[]{:S(2)}) copy-start(f32[128,1536]{1,0:T(8,128)} %rows_ref.3) | copy-start | bytes 2359300
  23.8 4.1 %copy-start.14 = (f32[1536]{0:T(1024)S(1)}, f32[1536]{0:T(1024)}, u32[]{:S(2)}) copy-start(f32[1536]{0:T(1024)} %param.19) | copy-start | bytes 18436
  24.8 8.0 %copy-start.1 = (f32[128,128]{1,0:T(8,128)}, f32[128,128]{1,0:T(8,128)S(1)}, u32[]{:S(2)}) copy-start(f32[128,128]{1,0:T(8,128)S(1)} %get-tuple-element.9.heat_ref) | copy-start | bytes 196612
  24.9 3.2 %copy-start.12 = (f32[4608]{0:T(1024)S(1)}, f32[4608]{0:T(1024)}, u32[]{:S(2)}) copy-start(f32[4608]{0:T(1024)} %param.22) | copy-start | bytes 55300
  24.9 4.5 %collective-permute-start = (f32[32,1536]{1,0:T(8,128)S(1)}, f32[32,1536]{1,0:T(8,128)S(1)}, u32[]{:S(2)}, u32[]{:S(2)}) collective-permute-start(f32[32,1536]{1,0:T(8,128)S(1)} %get-tuple-element.10), channel_id=1, source_target_pairs={{0,1},{1,2},{2,3},{3,4},{4,5},{5,6},{6,7},{7,8},{8,9},{9,10},{10,1... | collective-permute-start | bytes 589832 | tf_op jit(solution)/shard_map/ppermute | solution.py:278
  26.7 3.8 %collective-permute-start.1 = (f32[32,1536]{1,0:T(8,128)S(1)}, f32[32,1536]{1,0:T(8,128)S(1)}, u32[]{:S(2)}, u32[]{:S(2)}) collective-permute-start(f32[32,1536]{1,0:T(8,128)S(1)} %get-tuple-element.11), channel_id=1, source_target_pairs={{1,0},{2,1},{3,2},{4,3},{5,4},{6,5},{7,6},{8,7},{9,8},{10,9},{11,1... | collective-permute-start | bytes 589832 | tf_op jit(solution)/shard_map/ppermute | solution.py:279
  28.0 0.7 copy-start.13
  28.7 1.8 %copy-start.3 = (f32[6,128]{1,0:T(8,128)S(1)}, f32[6,128]{1,0:T(8,128)}, u32[]{:S(2)}) copy-start(f32[6,128]{1,0:T(8,128)} %factor_ref.1) | copy-start | bytes 9220
  29.3 1.1 %copy-start.2 = (s32[6,128]{1,0:T(8,128)S(1)}, s32[6,128]{1,0:T(8,128)}, u32[]{:S(2)}) copy-start(s32[6,128]{1,0:T(8,128)} %adjacent_ref.1) | copy-start | bytes 9220
  30.5 0.7 copy-start.7
  30.5 0.7 copy-start.8
  32.9 8.8 %copy-start.10 = (s32[2,4608]{1,0:T(2,128)S(1)}, s32[2,4608]{1,0:T(2,128)}, u32[]{:S(2)}) copy-start(s32[2,4608]{1,0:T(2,128)} %param.25) | copy-start | bytes 110596
  32.9 8.8 %copy-start.11 = (s32[2,4608]{1,0:T(2,128)S(1)}, s32[2,4608]{1,0:T(2,128)}, u32[]{:S(2)}) copy-start(s32[2,4608]{1,0:T(2,128)} %param.24) | copy-start | bytes 110596
  32.9 22.6 %all-to-all-start.1 = ((f32[32,2,1664]{2,1,0:T(2,128)}), f32[32,2,1664]{2,1,0:T(2,128)S(1)}, u32[]{:S(2)}, u32[]{:S(2)}) async-start(f32[32,2,1664]{2,1,0:T(2,128)} %get-tuple-element.13), calls=%async_computation.1 | async-start | bytes 851968 | tf_op jit(solution)/shard_map/all_to_all | solution.py:266
  55.4 0.8 copy-start.9

commit v2 on v1

v2 whole, which is shorter than its diff:
```python
import functools

import jax
import jax.numpy as jnp
from jax import lax
from jax.experimental import pallas as pl
from jax.experimental.pallas import tpu as pltpu
from jax.sharding import PartitionSpec as P

NEWTON = 2
HALO = 32
CAP = 2
EXTRA = 128

time_step = 0.5

f32 = jnp.float32
bf16 = jnp.bfloat16
i32 = jnp.int32
i16 = jnp.int16

VMEM = pl.BlockSpec(memory_space=pltpu.VMEM)
SMEM = pl.BlockSpec(memory_space=pltpu.SMEM)
HBM = pl.BlockSpec(memory_space=pltpu.HBM)
ANY = pl.BlockSpec(memory_space=pl.ANY)


def iota(shape, dim):
    return lax.broadcasted_iota(i32, shape, dim)


def column(row):
    n = row.shape[1]
    eye = iota((n, n), 0) == iota((n, n), 1)
    return jnp.sum(jnp.where(eye, row, jnp.zeros_like(row)), axis=1, keepdims=True)


def split3(x):
    hi = x.astype(bf16)
    rest = x - hi.astype(f32)
    mid = rest.astype(bf16)
    lo = (rest - mid.astype(f32)).astype(bf16)
    return hi, mid, lo


def pick(choice, rows, dims=(((1,), (0,)), ((), ()))):
    choice = choice.astype(bf16)
    out = None
    for part in split3(rows):
        term = lax.dot_general(choice, part, dims, preferred_element_type=f32)
        out = term if out is None else out + term
    return out


def send_choice(owner, me, partners):
    n = owner.shape[1]
    hits = ((iota((partners, n), 0) == owner) & (owner != me)).astype(f32)
    before = (iota((n, n), 0) < iota((n, n), 1)).astype(bf16)
    earlier = jnp.dot(hits.astype(bf16), before, preferred_element_type=f32)
    within = jnp.sum(earlier * hits, axis=0, keepdims=True).astype(i32)
    position = jnp.where(owner != me, owner * CAP + within, -1)
    return (iota((partners * CAP, n), 0) == position).astype(f32)


def in_hbm(*arrays):
    return tuple(pltpu.with_memory_space_constraint(x, pltpu.HBM) for x in arrays)


def begin(sources, targets, sems):
    copies = [
        pltpu.make_async_copy(source, target, sems.at[i])
        for i, (source, target) in enumerate(zip(sources, targets))
    ]
    for copy in copies:
        copy.start()
    return copies


def finish(copies):
    for copy in copies:
        copy.wait()


def beside_rows(values):
    n = values[0].shape[1]
    lane = iota((n, EXTRA), 1)
    out = jnp.zeros((n, EXTRA), f32)
    for i, value in enumerate(values):
        out = jnp.where(lane == i, column(value.astype(f32)), out)
    return out


def flat(ref):
    return jnp.concatenate([ref[q : q + 1, :] for q in range(ref.shape[0])], axis=1)


def arrived(recv_ref, places, n):
    partners, cap, width = recv_ref.shape
    got = recv_ref[...].reshape(partners * cap, width)
    land = (iota((partners * cap, n), 1) == places.astype(i32) - 1).astype(f32)
    return pick(land, got, (((0,), (0,)), ((), ())))


def stay_choice(owner, slot, me):
    n = owner.shape[1]
    return ((iota((n, n), 0) == slot) & (owner == me)).astype(f32)


def pack_kernel(
    me_ref,
    rows_hbm,
    temper_hbm,
    owner_hbm,
    slot_hbm,
    next_owner_hbm,
    next_slot_hbm,
    send_ref,
    rows,
    temper,
    owner,
    slot,
    next_owner,
    next_slot,
    sems,
):
    sources = (temper_hbm, owner_hbm, slot_hbm, next_owner_hbm, next_slot_hbm, rows_hbm)
    copies = begin(sources, (temper, owner, slot, next_owner, next_slot, rows), sems)
    finish(copies[:-1])
    partners, cap, _ = send_ref.shape
    species = rows.shape[1]
    choice = send_choice(owner[...], me_ref[0], partners)
    next_choice = send_choice(next_owner[...], me_ref[0], partners)
    none = jnp.zeros_like(temper[...])
    beside = pick(choice, beside_rows((temper[...], slot[...] + 1, none))) + pick(
        next_choice, beside_rows((none, none, next_slot[...] + 1))
    )
    send_ref[:, :, species:] = beside.reshape(partners, cap, EXTRA)
    finish(copies[-1:])
    send_ref[:, :, :species] = pick(choice, rows[...]).reshape(partners, cap, species)


def prepare_kernel(
    me_ref,
    rows_hbm,
    temper_hbm,
    owner_hbm,
    slot_hbm,
    next_owner_hbm,
    adjacent_hbm,
    factor_hbm,
    coefficient_hbm,
    frequency_hbm,
    energy_hbm,
    consumed_hbm,
    after_ref,
    state_ref,
    heat_ref,
    choice_ref,
    weight_hi_ref,
    weight_mid_ref,
    scale_ref,
    total_ref,
    frequency_ref,
    energy_ref,
    consumed_ref,
    rows,
    temper,
    owner,
    slot,
    next_owner,
    adjacent,
    factor,
    coefficient,
    frequency,
    energy,
    sems,
):
    sources = (temper_hbm, owner_hbm, slot_hbm, next_owner_hbm, adjacent_hbm, factor_hbm)
    sources += (coefficient_hbm, frequency_hbm, energy_hbm, consumed_hbm, rows_hbm)
    targets = (temper, owner, slot, next_owner, adjacent, factor)
    targets += (coefficient, frequency, energy, consumed_ref, rows)
    copies = begin(sources, targets, sems)
    finish(copies[:-1])
    me = me_ref[0]
    choice_ref[...] = send_choice(next_owner[...], me, choice_ref.shape[0] // CAP)
    weight, total = face_weights(me, adjacent[...], factor[...])
    weight_hi_ref[...], weight_mid_ref[...], _ = split3(weight)
    scale_ref[...] = time_step * flat(coefficient)
    total_ref[...] = jnp.broadcast_to(column(total), total_ref.shape)
    frequency_ref[...] = flat(frequency)
    energy_ref[...] = flat(energy)
    stay = stay_choice(owner[...], slot[...], me)
    heat_ref[...] = pick(stay, jnp.broadcast_to(column(temper[...]), heat_ref.shape))
    finish(copies[-1:])
    state_ref[...] = pick(stay, rows[...])


def flow_kernel(
    me_ref,
    recv_ref,
    state_ref,
    temper_ref,
    after_ref,
    flow_ref,
    heat_ref,
    inner_ref,
    outer_ref,
    place_ref,
):
    n, species = state_ref.shape
    partners, cap, width = recv_ref.shape
    beside = recv_ref[:, :, species:].reshape(partners * cap, EXTRA)
    rows = arrived(recv_ref, beside[:, 1:2], n)
    state = rows[:, :species] + state_ref[...]
    flow_ref[...] = state
    heat_ref[...] = rows[:, species:] + temper_ref[...]
    place_ref[...] = jnp.broadcast_to(beside[:, 2:3], place_ref.shape)
    even = lax.rem(me_ref[0], 2) == 0
    inner_ref[...] = jnp.where(even, state[n - HALO :], state[:HALO])
    outer_ref[...] = jnp.where(even, state[:HALO], state[n - HALO :])


def face_weights(me, adjacent, factor):
    n = adjacent.shape[1]
    index = adjacent - me * n + HALO
    rows = iota((n + 2 * HALO, n), 0)
    weight = jnp.zeros((n + 2 * HALO, n), f32)
    total = jnp.zeros((1, n), f32)
    for face in range(adjacent.shape[0]):
        weight += jnp.where(rows == index[face : face + 1], factor[face : face + 1], 0.0)
        total += factor[face : face + 1]
    return weight, total


def table(index_iota, first, second):
    one, zero = jnp.ones((), bf16), jnp.zeros((), bf16)
    return jnp.where(index_iota == first, one, zero) + jnp.where(index_iota == second, one, zero)


def largest(total, *wanted):
    return next(b for b in wanted if total % b == 0)


def column_table(pairs):
    block = pairs.shape[1]
    columns = jnp.transpose(
        jnp.concatenate([pairs, jnp.zeros((6, block), i32)], axis=0)
    ).astype(i16)

    def rows(species):
        return table(
            iota((block, species), 1).astype(i16), columns[:, 0:1], columns[:, 1:2]
        )

    return rows


def product_kernel(yielded_ref, after_ref, product_t_ref, done_ref):
    product_t_ref[...] = column_table(yielded_ref[...])(product_t_ref.shape[1])
    done_ref[...] = jnp.zeros_like(done_ref)


def react_kernel(
    consumed_ref, product_t_hbm, after_ref, react_ref, react_t_ref, product_t_ref, sems
):
    copies = begin((product_t_hbm,), (product_t_ref,), sems)
    species, reactions = react_ref.shape
    block = largest(reactions, 512, 256, 128)
    down_species = iota((species, block), 0).astype(i16)

    def fill(b, carry):
        at = pl.ds(pl.multiple_of(b * block, block), block)
        used = consumed_ref[:, at]
        react_ref[:, at] = table(down_species, used[0:1].astype(i16), used[1:2].astype(i16))
        return carry

    def fill_t(b, carry):
        at = pl.ds(pl.multiple_of(b * block, block), block)
        react_t_ref[at, :] = column_table(consumed_ref[:, at])(species)
        return carry

    lax.fori_loop(0, reactions // block, fill, 0)
    lax.fori_loop(0, reactions // block, fill_t, 0, unroll=largest(reactions // block, 3, 2, 1))
    finish(copies)


def chemistry_kernel(
    me_ref,
    flow_ref,
    heat_ref,
    inner_ref,
    outer_ref,
    react_ref,
    react_t_ref,
    product_t_ref,
    choice_ref,
    weight_hi_ref,
    weight_mid_ref,
    scale_ref,
    total_ref,
    frequency_ref,
    energy_ref,
    spread_ref,
    chem_ref,
    send_ref,
    rate_ref,
    log_ref,
):
    flow = flow_ref[...]
    even = lax.rem(me_ref[0], 2) == 0
    inner, outer = inner_ref[...], outer_ref[...]
    extended = jnp.concatenate(
        [jnp.where(even, outer, inner), flow, jnp.where(even, inner, outer)], axis=0
    )
    e_hi, e_mid, _ = split3(extended)
    dims = (((0,), (0,)), ((), ()))
    coupling = (
        lax.dot_general(weight_hi_ref[...], e_hi, dims, preferred_element_type=f32)
        + lax.dot_general(weight_hi_ref[...], e_mid, dims, preferred_element_type=f32)
        + lax.dot_general(weight_mid_ref[...], e_hi, dims, preferred_element_type=f32)
    )
    scale = scale_ref[...]
    spread = (flow + scale * coupling) / (1.0 + scale * total_ref[:, 0:1])
    spread_ref[...] = spread
    chem_ref[...] = spread
    inverse = 1.0 / heat_ref[:, 0:1]
    species, reactions = react_ref.shape
    across = largest(reactions, 512, 256, 128)
    down = largest(species, 512, 256, 128)
    tiles = [slice(first, first + down) for first in range(0, species, down)]

    for turn in range(NEWTON):
        log_ref[...] = jnp.log(chem_ref[...]).astype(bf16)
        for first in range(0, reactions, across):
            at = slice(first, first + across)
            exponent = jnp.dot(log_ref[...], react_ref[:, at], preferred_element_type=f32)
            log_rate = frequency_ref[:, at] - energy_ref[:, at] * inverse
            rate_ref[:, at] = jnp.exp(log_rate + exponent).astype(bf16)
        for at in tiles:
            loss = jnp.dot(rate_ref[...], react_t_ref[:, at], preferred_element_type=f32)
            gain = jnp.dot(rate_ref[...], product_t_ref[:, at], preferred_element_type=f32)
            chem_ref[:, at] = (spread_ref[:, at] + time_step * gain) / (
                1.0 + time_step * loss / chem_ref[:, at]
            )
    send_ref[...] = pick(choice_ref[...], chem_ref[...]).reshape(send_ref.shape)


def stay_kernel(me_ref, rows_ref, owner_ref, slot_ref, out_ref):
    out_ref[...] = pick(stay_choice(owner_ref[...], slot_ref[...], me_ref[0]), rows_ref[...])


def land_kernel(recv_ref, place_ref, stay_ref, out_ref):
    out_ref[...] = arrived(recv_ref, place_ref[:, 0:1], out_ref.shape[0]) + stay_ref[...]


def call(kernel, inputs, specs, outputs, scratch=(), limit=6, cost=None):
    outputs = tuple(jax.ShapeDtypeStruct(o, f32) if isinstance(o, tuple) else o for o in outputs)
    return pl.pallas_call(
        kernel,
        out_shape=outputs,
        in_specs=specs,
        out_specs=tuple([VMEM] * len(outputs)),
        scratch_shapes=list(scratch),
        compiler_params=pltpu.CompilerParams(vmem_limit_bytes=limit * 2**20),
        cost_estimate=cost,
    )(*inputs)


def like(*arrays):
    return [pltpu.VMEM(x.shape, x.dtype) for x in arrays], pltpu.SemaphoreType.DMA((len(arrays),))


def table_cost(species, reactions, tables):
    return pl.CostEstimate(
        flops=40 * species * reactions * tables,
        bytes_accessed=2 * species * reactions * tables,
        transcendentals=0,
    )


def local(
    earlier_kinetics_concentrations,
    thermal_level,
    earlier_fluid_holder,
    earlier_fluid_slot,
    adjacent_volumes,
    interface_spreading_factor,
    species_spreading_coefficient,
    present_kinetics_holder,
    present_kinetics_slot,
    natural_frequency_factor,
    arrhenius_energy,
    consumed_species,
    yielded_species,
):
    n, species = earlier_kinetics_concentrations.shape
    reactions = natural_frequency_factor.shape[0]
    partners = lax.axis_size("cells")
    me = lax.axis_index("cells").astype(i32).reshape(1)
    row = lambda x: x.reshape(1, -1)

    def exchange(x):
        return lax.all_to_all(x, "cells", split_axis=0, concat_axis=0, tiled=True)

    earlier = (
        earlier_kinetics_concentrations,
        row(thermal_level),
        row(earlier_fluid_holder),
        row(earlier_fluid_slot),
    )
    owner, slot = row(present_kinetics_holder), row(present_kinetics_slot)
    pack_scratch, pack_sems = like(*earlier, owner, slot)
    (send,) = call(
        pack_kernel,
        (me, *in_hbm(*earlier, owner, slot)),
        [SMEM] + [HBM] * 6,
        ((partners, CAP, species + EXTRA),),
        [*pack_scratch, pack_sems],
    )

    block = largest(reactions, 512, 256, 128)
    product_t, done = pl.pallas_call(
        product_kernel,
        grid=(reactions // block,),
        out_shape=(
            pltpu.HBM((reactions, species), bf16),
            jax.ShapeDtypeStruct((8, 128), f32),
        ),
        in_specs=[pl.BlockSpec((2, block), lambda b: (0, b)), ANY],
        out_specs=(
            pl.BlockSpec((block, species), lambda b: (b, 0)),
            pl.BlockSpec((8, 128), lambda b: (0, 0)),
        ),
        compiler_params=pltpu.CompilerParams(vmem_limit_bytes=16 * 2**20),
        cost_estimate=table_cost(species, reactions, 1),
    )(*in_hbm(yielded_species), send)

    recv = exchange(send)
    ready = (
        owner,
        adjacent_volumes,
        interface_spreading_factor,
        species_spreading_coefficient.reshape(-1, 128),
        natural_frequency_factor.reshape(-1, 128),
        arrhenius_energy.reshape(-1, 128),
    )
    ready_scratch, _ = like(*earlier, *ready)
    state, heat, *prepared, consumed = call(
        prepare_kernel,
        (me, *in_hbm(*earlier, *ready, consumed_species), send),
        [SMEM] + [HBM] * 11 + [ANY],
        (
            (n, species),
            (n, EXTRA),
            (partners * CAP, n),
            jax.ShapeDtypeStruct((n + 2 * HALO, n), bf16),
            jax.ShapeDtypeStruct((n + 2 * HALO, n), bf16),
            (1, species),
            (n, 128),
            (1, reactions),
            (1, reactions),
            jax.ShapeDtypeStruct((2, reactions), i32),
        ),
        [*ready_scratch, pltpu.SemaphoreType.DMA((11,))],
    )
    flow, heat, to_inner, to_outer, place = call(
        flow_kernel,
        (me, recv, state, heat, done),
        [SMEM] + [VMEM] * 3 + [ANY],
        ((n, species), (n, EXTRA), (HALO, species), (HALO, species), (partners * CAP, EXTRA)),
    )
    inner = [(i, i ^ 1) for i in range(partners)]
    outer = [(i, ((i + 1) ^ 1) - 1) for i in range(1, partners - 1)]
    from_outer = lax.ppermute(to_outer, "cells", outer)
    from_inner = lax.ppermute(to_inner, "cells", inner)
    tables = call(
        react_kernel,
        (consumed, *in_hbm(product_t), heat),
        [VMEM, HBM, ANY],
        (
            jax.ShapeDtypeStruct((species, reactions), bf16),
            jax.ShapeDtypeStruct((reactions, species), bf16),
            jax.ShapeDtypeStruct((reactions, species), bf16),
        ),
        [pltpu.SemaphoreType.DMA((1,))],
        limit=4,
        cost=table_cost(species, reactions, 2),
    )
    spread, chem, send = call(
        chemistry_kernel,
        (me, flow, heat, from_inner, from_outer, *tables, *prepared),
        [SMEM] + [VMEM] * (7 + len(prepared)),
        ((n, species), (n, species), (partners, CAP, species)),
        [pltpu.VMEM((n, reactions), bf16), pltpu.VMEM((n, species), bf16)],
        limit=6,
    )
    recv = exchange(send)
    (stay,) = call(stay_kernel, (me, chem, owner, slot), [SMEM] + [VMEM] * 3, ((n, species),))
    (chem_next,) = call(land_kernel, (recv, place, stay), [VMEM] * 3, ((n, species),))
    return (spread, chem_next)


def solution(mesh):
    in_specs = (
        P("cells", None),
        P("cells"),
        P("cells"),
        P("cells"),
        P(None, "cells"),
        P(None, "cells"),
        P(),
        P("cells"),
        P("cells"),
        P(),
        P(),
        P(),
        P(),
    )
    out_specs = (P("cells", None), P("cells", None))
    return jax.shard_map(local, mesh=mesh, in_specs=in_specs, out_specs=out_specs, check_vma=False)
```

time: 81 us -> 66 us (0.81)
  blocking collectives: 20.9 us -> 0 us
  Pallas kernels: 27.6 us -> 36.4 us
  local copies, waits for them, and re-layouts: 4.59 us -> 0.01 us
  waiting for transfers between devices: 14.1 us -> 15.6 us
  starting transfers between devices: 11.8 us -> 12.9 us
    all_to_all x1 -> x0, blocking collectives: 20.9 us -> none  [exchange(): return lax.all_to_all(x, 'cells', split_axis=0, concat_axis=0, tiled=True)]
    pallas_call x4 -> x8, Pallas kernels: 27.6 us -> 36.4 us  [the longest x7 27.4 us: call(): pl.pallas_call(kernel, out_shape=outputs, in_specs=specs, out_specs=tuple...]
    all_to_all x1 -> x2, starting transfers between devices: 8.77 us -> 12.1 us  [exchange(): return lax.all_to_all(x, 'cells', split_axis=0, concat_axis=0, tiled=True)]
    unnamed x30 -> x4, local copies, waits for them, and re-layouts: 3.28 us -> 0.01 us
    all_to_all x1 -> x2, waiting for transfers between devices: 13 us -> 15.6 us  [exchange(): return lax.all_to_all(x, 'cells', split_axis=0, concat_axis=0, tiled=True)]
    ppermute x2, starting transfers between devices: 3.07 us -> 0.74 us  [the longest x1 0.67 us: local(): from_outer = lax.ppermute(to_outer, 'cells', outer)]
    reshape x3 -> x0, local copies, waits for them, and re-layouts: 1.24 us -> none  [local(): row = lambda x: x.reshape(1, -1)]
    ppermute x2, waiting for transfers between devices: 1.12 us -> 0.01 us  [the longest x1 0.01 us: local(): from_inner = lax.ppermute(to_inner, 'cells', inner)]
  transfers between devices with their start and end apart: 3 -> 4, of which waited for: 2 -> 2; matrix products, arithmetic and copies ran while one was open for 3% -> 0% of each run, Pallas kernels for 0% -> 28%
where the time goes in v2:
time: 66 us; the launch traced here: 65.6 us
  Pallas kernels  36.4 us (55%)
  waiting for transfers between devices  15.6 us (24%)
  starting transfers between devices  12.9 us (20%)
  between operations  0.75 us (1%)
    pallas_call x7, Pallas kernels, call(): pl.pallas_call(kernel, out_shape=outputs, in_specs=specs, out_specs=tuple...  27.4 us
    all_to_all x2, waiting for transfers between devices, exchange(): return lax.all_to_all(x, 'cells', split_axis=0, concat_axis=0, tiled=True)  15.6 us
    all_to_all x2, starting transfers between devices, exchange(): return lax.all_to_all(x, 'cells', split_axis=0, concat_axis=0, tiled=True)  12.1 us
    pallas_call x1, Pallas kernels, local(): pl.pallas_call(product_kernel, grid=(reactions // block,), out_shape=(plt...  8.93 us
  transfers between devices with their start and end apart: 4, of which 2 were waited for; matrix products, arithmetic and copies ran while one was open for 0% of the time, Pallas kernels for 28%

profile of v2, /device:TPU:0, one launch (start us, length us, event | category | flops | bytes accessed | tf_op | source)
XLA Modules:
  0.0 65.6 jit_solution(13719899241667148794)
XLA Ops:
  0.6 2.4 %shard_map.140.after_ref = f32[32,2,1664]{2,1,0:T(2,128)} custom-call(s32[1]{0:T(128)} %bitcast.me_ref, f32[128,1536]{1,0:T(8,128)} %rows_hbm.3, f32[1,128]{1,0:T(1,128)} %bitcast.17, s32[1,128]{1,0:T(1,128)} %bitcast.19, s32[1,128]{1,0:T(1,128)} %bitcast.21, s32[1,128]{1,0:T(1,128)} %bitcast.9, s32[1,128]{1,0:T(1,128)} %bitcast.12), custom_call_target="tpu_custom_call" | custom-call | tf_op jit(solution)/shard_map/pallas_call | solution.py:358
  3.0 7.3 %all-to-all-start = ((f32[32,2,1664]{2,1,0:T(2,128)}), f32[32,2,1664]{2,1,0:T(2,128)S(1)}, u32[]{:S(2)}, u32[]{:S(2)}) async-start(f32[32,2,1664]{2,1,0:T(2,128)} %shard_map.140.after_ref), calls=%async_computation | async-start | bytes 851968 | tf_op jit(solution)/shard_map/all_to_all | solution.py:403
  10.3 1.9 %shard_map.141 = (f32[128,1536]{1,0:T(8,128)S(1)}, f32[128,128]{1,0:T(8,128)S(1)}, f32[64,128]{1,0:T(8,128)S(1)}, bf16[192,128]{1,0:T(8,128)(2,1)S(1)}, bf16[192...) custom-call(s32[1]{0:T(128)} %bitcast.me_ref, ...), custom_call_target="tpu_custom_call" | custom-call | tf_op jit(solution)/shard_map/pallas_call | solution.py:358
  12.3 8.9 %shard_map.142 = (bf16[4608,1536]{1,0:T(8,128)(2,1)}, f32[8,128]{1,0:T(8,128)S(1)}) custom-call(s32[2,4608]{1,0:T(2,128)} %yielded_ref.1, f32[32,2,1664]{2,1,0:T(2,128)} %shard_map.140.after_ref), custom_call_target="tpu_custom_call" | custom-call | flops 283115520 | bytes 14155776 | tf_op jit(solution)/shard_map/pallas_call | solution.py:422
  21.2 2.9 %all-to-all-done.recv_ref = f32[32,2,1664]{2,1,0:T(2,128)S(1)} async-done(((f32[32,2,1664]{2,1,0:T(2,128)}), f32[32,2,1664]{2,1,0:T(2,128)S(1)}, u32[]{:S(2)}, u32[]{:S(2)}) %all-to-all-start) | async-done | bytes 426016 | tf_op jit(solution)/shard_map/all_to_all | solution.py:403
  24.1 0.7 %shard_map.143 = (f32[128,1536]{1,0:T(8,128)S(1)}, f32[128,128]{1,0:T(8,128)S(1)}, f32[32,1536]{1,0:T(8,128)S(1)}, f32[32,1536]{1,0:T(8,128)S(1)}, f32[64,128]{1,0:T(8,128)S(1)}) custom-call(s32[1]{0:T(128)} %bitcast.me_ref, f32[32,2,1664]{2,1,0:T(2,128)S(1)} %all-to-all-done.recv_ref, f32[128,1536]{1,0:T(8,128)S(1)} %get-tuple-element.25.state_ref, ...), custom_call_target="tpu_custom_call" | custom-call | tf_op jit(solution)/shard_map/pallas_call | solution.py:358
  24.8 0.1 collective-permute-start
  24.9 0.7 %collective-permute-start.1 = (f32[32,1536]{1,0:T(8,128)S(1)}, f32[32,1536]{1,0:T(8,128)S(1)}, u32[]{:S(2)}, u32[]{:S(2)}) collective-permute-start(f32[32,1536]{1,0:T(8,128)S(1)} %get-tuple-element.31), channel_id=1, source_target_pairs={{1,2},{2,1},{3,4},{4,3},{5,6},{6,5},{7,8},{8,7},{9,10},{10,9},{11,... | collective-permute-start | bytes 589832 | tf_op jit(solution)/shard_map/ppermute | solution.py:474
  25.6 6.9 %shard_map.144 = (bf16[1536,4608]{1,0:T(8,128)(2,1)S(1)}, bf16[4608,1536]{1,0:T(8,128)(2,1)S(1)}, bf16[4608,1536]{1,0:T(8,128)(2,1)S(1)}) custom-call(s32[2,4608]{1,0:T(2,128)S(1)} %get-tuple-element.32.consumed_ref, bf16[4608,1536]{1,0:T(8,128)(2,1)} %get-tuple-element.33.product_t_hbm, f32[128,128]{1,0:T(8,128)S(1)} %get-tuple-element.29.after_ref.heat_ref), custom_call_target="tpu_custom_call" | custom-call | flops 566231040 | bytes 28311552 | tf_op jit(solution)/shard_map/pallas_call | solution.py:358
  32.4 0.0 collective-permute-done.inner_ref
  32.4 0.0 collective-permute-done.1.outer_ref
  32.5 0.0 copy-start
  32.5 0.0 copy-start.1
  32.5 13.6 %shard_map.145 = (f32[128,1536]{1,0:T(8,128)}, f32[128,1536]{1,0:T(8,128)S(1)}, f32[32,2,1536]{2,1,0:T(2,128)}) custom-call(s32[1]{0:T(128)} %bitcast.me_ref, f32[128,1536]{1,0:T(8,128)S(1)} %get-tuple-element.28.flow_ref, f32[128,128]{1,0:T(8,128)S(1)} %get-tuple-element.29.after_ref.heat_ref, f32[32,1536]{1,0:T(8,128)S(1)} %collective-permute-done.inner_ref, ...), custom_call_target="tpu_custom_call" | custom-call | tf_op jit(solution)/shard_map/pallas_call | solution.py:358
  46.1 4.8 %all-to-all-start.1 = ((f32[32,2,1536]{2,1,0:T(2,128)}), f32[32,2,1536]{2,1,0:T(2,128)S(1)}, u32[]{:S(2)}, u32[]{:S(2)}) async-start(f32[32,2,1536]{2,1,0:T(2,128)} %get-tuple-element.45), calls=%async_computation.1 | async-start | bytes 786432 | tf_op jit(solution)/shard_map/all_to_all | solution.py:403
  50.9 0.0 copy-done
  50.9 0.0 copy-done.1
  50.9 0.5 shard_map.146.stay_ref
  51.4 12.7 %all-to-all-done.1.recv_ref = f32[32,2,1536]{2,1,0:T(2,128)S(1)} async-done(((f32[32,2,1536]{2,1,0:T(2,128)}), f32[32,2,1536]{2,1,0:T(2,128)S(1)}, u32[]{:S(2)}, u32[]{:S(2)}) %all-to-all-start.1) | async-done | bytes 393248 | tf_op jit(solution)/shard_map/all_to_all | solution.py:403
  64.1 1.5 %shard_map.147 = f32[128,1536]{1,0:T(8,128)} custom-call(f32[32,2,1536]{2,1,0:T(2,128)S(1)} %all-to-all-done.1.recv_ref, f32[64,128]{1,0:T(8,128)S(1)} %get-tuple-element.46.place_ref, f32[128,1536]{1,0:T(8,128)S(1)} %shard_map.146.stay_ref), custom_call_target="tpu_custom_call" | custom-call | tf_op jit(solution)/shard_map/pallas_call | solution.py:358
Async XLA Ops:
  3.0 21.1 %all-to-all-start = ((f32[32,2,1664]{2,1,0:T(2,128)}), f32[32,2,1664]{2,1,0:T(2,128)S(1)}, u32[]{:S(2)}, u32[]{:S(2)}) async-start(f32[32,2,1664]{2,1,0:T(2,128)} %shard_map.140.after_ref), calls=%async_computation | async-start | bytes 851968 | tf_op jit(solution)/shard_map/all_to_all | solution.py:403
  24.8 7.6 %collective-permute-start = (f32[32,1536]{1,0:T(8,128)S(1)}, f32[32,1536]{1,0:T(8,128)S(1)}, u32[]{:S(2)}, u32[]{:S(2)}) collective-permute-start(f32[32,1536]{1,0:T(8,128)S(1)} %get-tuple-element.30), channel_id=1, source_target_pairs={{0,1},{1,0},{2,3},{3,2},{4,5},{5,4},{6,7},{7,6},{8,9},{9,8},{10,11... | collective-permute-start | bytes 589832 | tf_op jit(solution)/shard_map/ppermute | solution.py:475
  24.9 7.6 %collective-permute-start.1 = (f32[32,1536]{1,0:T(8,128)S(1)}, f32[32,1536]{1,0:T(8,128)S(1)}, u32[]{:S(2)}, u32[]{:S(2)}) collective-permute-start(f32[32,1536]{1,0:T(8,128)S(1)} %get-tuple-element.31), channel_id=1, source_target_pairs={{1,2},{2,1},{3,4},{4,3},{5,6},{6,5},{7,8},{8,7},{9,10},{10,9},{11,... | collective-permute-start | bytes 589832 | tf_op jit(solution)/shard_map/ppermute | solution.py:474
  32.5 18.5 %copy-start = (s32[128]{0:T(128)S(1)}, s32[128]{0:T(128)}, u32[]{:S(2)}) copy-start(s32[128]{0:T(128)} %param.20) | copy-start | bytes 1540
  32.5 18.5 %copy-start.1 = (s32[128]{0:T(128)S(1)}, s32[128]{0:T(128)}, u32[]{:S(2)}) copy-start(s32[128]{0:T(128)} %param.21) | copy-start | bytes 1540
  46.1 18.0 %all-to-all-start.1 = ((f32[32,2,1536]{2,1,0:T(2,128)}), f32[32,2,1536]{2,1,0:T(2,128)S(1)}, u32[]{:S(2)}, u32[]{:S(2)}) async-start(f32[32,2,1536]{2,1,0:T(2,128)} %get-tuple-element.45), calls=%async_computation.1 | async-start | bytes 786432 | tf_op jit(solution)/shard_map/all_to_all | solution.py:403

commit v3 on v2

--- a/solution.py
+++ b/solution.py
@@ -29,27 +29,27 @@
     return lax.broadcasted_iota(i32, shape, dim)
 
 
+def largest(total, *wanted):
+    return next(b for b in wanted if total % b == 0)
+
+
 def column(row):
     n = row.shape[1]
     eye = iota((n, n), 0) == iota((n, n), 1)
     return jnp.sum(jnp.where(eye, row, jnp.zeros_like(row)), axis=1, keepdims=True)
 
 
-def split3(x):
+def split(x):
     hi = x.astype(bf16)
-    rest = x - hi.astype(f32)
-    mid = rest.astype(bf16)
-    lo = (rest - mid.astype(f32)).astype(bf16)
-    return hi, mid, lo
+    return hi, (x - hi.astype(f32)).astype(bf16)
 
 
 def pick(choice, rows, dims=(((1,), (0,)), ((), ()))):
     choice = choice.astype(bf16)
-    out = None
-    for part in split3(rows):
-        term = lax.dot_general(choice, part, dims, preferred_element_type=f32)
-        out = term if out is None else out + term
-    return out
+    hi, mid = split(rows)
+    return lax.dot_general(choice, hi, dims, preferred_element_type=f32) + lax.dot_general(
+        choice, mid, dims, preferred_element_type=f32
+    )
 
 
 def send_choice(owner, me, partners):
@@ -76,6 +76,17 @@
     return copies
 
 
+def pieces(total):
+    width = largest(total, 768, 512, 256, 128)
+    return [slice(first, first + width) for first in range(0, total, width)]
+
+
+def leave(source, target, sem):
+    copy = pltpu.make_async_copy(source, target, sem)
+    copy.start()
+    return copy
+
+
 def finish(copies):
     for copy in copies:
         copy.wait()
@@ -94,11 +105,14 @@
     return jnp.concatenate([ref[q : q + 1, :] for q in range(ref.shape[0])], axis=1)
 
 
+def landing(places, n):
+    return (iota((places.shape[0], n), 1) == places.astype(i32) - 1).astype(f32)
+
+
 def arrived(recv_ref, places, n):
     partners, cap, width = recv_ref.shape
     got = recv_ref[...].reshape(partners * cap, width)
-    land = (iota((partners * cap, n), 1) == places.astype(i32) - 1).astype(f32)
-    return pick(land, got, (((0,), (0,)), ((), ())))
+    return pick(landing(places, n), got, (((0,), (0,)), ((), ())))
 
 
 def stay_choice(owner, slot, me):
@@ -184,7 +198,7 @@
     me = me_ref[0]
     choice_ref[...] = send_choice(next_owner[...], me, choice_ref.shape[0] // CAP)
     weight, total = face_weights(me, adjacent[...], factor[...])
-    weight_hi_ref[...], weight_mid_ref[...], _ = split3(weight)
+    weight_hi_ref[...], weight_mid_ref[...] = split(weight)
     scale_ref[...] = time_step * flat(coefficient)
     total_ref[...] = jnp.broadcast_to(column(total), total_ref.shape)
     frequency_ref[...] = flat(frequency)
@@ -203,8 +217,8 @@
     after_ref,
     flow_ref,
     heat_ref,
+    outer_ref,
     inner_ref,
-    outer_ref,
     place_ref,
 ):
     n, species = state_ref.shape
@@ -237,10 +251,6 @@
     return jnp.where(index_iota == first, one, zero) + jnp.where(index_iota == second, one, zero)
 
 
-def largest(total, *wanted):
-    return next(b for b in wanted if total % b == 0)
-
-
 def column_table(pairs):
     block = pairs.shape[1]
     columns = jnp.transpose(
@@ -255,17 +265,62 @@
     return rows
 
 
-def product_kernel(yielded_ref, after_ref, product_t_ref, done_ref):
-    product_t_ref[...] = column_table(yielded_ref[...])(product_t_ref.shape[1])
+def product_kernel(
+    yielded_hbm,
+    consumed_hbm,
+    after_hbm,
+    product_t_hbm,
+    head_hbm,
+    done_ref,
+    yielded,
+    consumed,
+    product_t,
+    head,
+    sems,
+    out_sems,
+):
+    block, species = head.shape
+    blocks = product_t.shape[0] // block
+    finish(begin((yielded_hbm, consumed_hbm.at[:, :block]), (yielded, consumed), sems))
+
+    def out(b):
+        at = pl.ds(pl.multiple_of(b * block, block), block)
+        return pltpu.make_async_copy(
+            product_t.at[at, :], product_t_hbm.at[at, :], out_sems.at[b]
+        )
+
+    def fill(b, carry):
+        at = pl.ds(pl.multiple_of(b * block, block), block)
+        product_t[at, :] = column_table(yielded[:, at])(species)
+        out(b).start()
+        return carry
+
+    def drain(b, carry):
+        out(b).wait()
+        return carry
+
+    lax.fori_loop(0, blocks, fill, 0, unroll=largest(blocks, 3, 2, 1))
+    head[...] = column_table(consumed[...])(species)
+    left = leave(head, head_hbm, out_sems.at[blocks])
     done_ref[...] = jnp.zeros_like(done_ref)
+    lax.fori_loop(0, blocks, drain, 0)
+    left.wait()
 
 
 def react_kernel(
-    consumed_ref, product_t_hbm, after_ref, react_ref, react_t_ref, product_t_ref, sems
+    consumed_ref,
+    product_t_hbm,
+    head_hbm,
+    after_ref,
+    react_ref,
+    react_t_ref,
+    product_t_ref,
+    sems,
 ):
-    copies = begin((product_t_hbm,), (product_t_ref,), sems)
+    block = head_hbm.shape[0]
+    targets = (product_t_ref, react_t_ref.at[:block, :])
+    copies = begin((product_t_hbm, head_hbm), targets, sems)
     species, reactions = react_ref.shape
-    block = largest(reactions, 512, 256, 128)
     down_species = iota((species, block), 0).astype(i16)
 
     def fill(b, carry):
@@ -280,7 +335,8 @@
         return carry
 
     lax.fori_loop(0, reactions // block, fill, 0)
-    lax.fori_loop(0, reactions // block, fill_t, 0, unroll=largest(reactions // block, 3, 2, 1))
+    rest = reactions // block - 1
+    lax.fori_loop(1, rest + 1, fill_t, 0, unroll=largest(rest, 4, 3, 2, 1))
     finish(copies)
 
 
@@ -300,11 +356,14 @@
     total_ref,
     frequency_ref,
     energy_ref,
-    spread_ref,
+    spread_hbm,
     chem_ref,
-    send_ref,
+    send_hbm,
     rate_ref,
     log_ref,
+    spread_ref,
+    out_sems,
+    *out,
 ):
     flow = flow_ref[...]
     even = lax.rem(me_ref[0], 2) == 0
@@ -312,7 +371,7 @@
     extended = jnp.concatenate(
         [jnp.where(even, outer, inner), flow, jnp.where(even, inner, outer)], axis=0
     )
-    e_hi, e_mid, _ = split3(extended)
+    e_hi, e_mid = split(extended)
     dims = (((0,), (0,)), ((), ()))
     coupling = (
         lax.dot_general(weight_hi_ref[...], e_hi, dims, preferred_element_type=f32)
@@ -322,6 +381,7 @@
     scale = scale_ref[...]
     spread = (flow + scale * coupling) / (1.0 + scale * total_ref[:, 0:1])
     spread_ref[...] = spread
+    left = [leave(spread_ref, spread_hbm, out_sems.at[len(out)])]
     chem_ref[...] = spread
     inverse = 1.0 / heat_ref[:, 0:1]
     species, reactions = react_ref.shape
@@ -342,15 +402,25 @@
             chem_ref[:, at] = (spread_ref[:, at] + time_step * gain) / (
                 1.0 + time_step * loss / chem_ref[:, at]
             )
-    send_ref[...] = pick(choice_ref[...], chem_ref[...]).reshape(send_ref.shape)
-
-
-def stay_kernel(me_ref, rows_ref, owner_ref, slot_ref, out_ref):
+    for i, at in enumerate(pieces(species)):
+        out[i][...] = pick(choice_ref[...], chem_ref[:, at]).reshape(out[i].shape)
+        left.append(leave(out[i], send_hbm.at[:, :, at], out_sems.at[i]))
+    finish(left)
+
+
+def stay_kernel(me_ref, rows_ref, place_ref, owner_ref, slot_ref, out_ref, land_ref):
     out_ref[...] = pick(stay_choice(owner_ref[...], slot_ref[...], me_ref[0]), rows_ref[...])
-
-
-def land_kernel(recv_ref, place_ref, stay_ref, out_ref):
-    out_ref[...] = arrived(recv_ref, place_ref[:, 0:1], out_ref.shape[0]) + stay_ref[...]
+    land_ref[...] = jnp.transpose(landing(place_ref[:, 0:1], rows_ref.shape[0]))
+
+
+def land_kernel(recv_ref, land_ref, stay_ref, out_hbm, out_sems, *out):
+    partners, cap, species = recv_ref.shape
+    left = []
+    for i, at in enumerate(pieces(species)):
+        got = recv_ref[:, :, at].reshape(partners * cap, -1)
+        out[i][...] = pick(land_ref[...], got) + stay_ref[:, at]
+        left.append(leave(out[i], out_hbm.at[:, at], out_sems.at[i]))
+    finish(left)
 
 
 def call(kernel, inputs, specs, outputs, scratch=(), limit=6, cost=None):
@@ -359,7 +429,7 @@
         kernel,
         out_shape=outputs,
         in_specs=specs,
-        out_specs=tuple([VMEM] * len(outputs)),
+        out_specs=tuple(VMEM if isinstance(o, jax.ShapeDtypeStruct) else HBM for o in outputs),
         scratch_shapes=list(scratch),
         compiler_params=pltpu.CompilerParams(vmem_limit_bytes=limit * 2**20),
         cost_estimate=cost,
@@ -410,6 +480,8 @@
     )
     owner, slot = row(present_kinetics_holder), row(present_kinetics_slot)
     pack_scratch, pack_sems = like(*earlier, owner, slot)
+    parts = pieces(species)
+    parts_scratch = [pltpu.VMEM((partners, CAP, species // len(parts)), f32) for _ in parts]
     (send,) = call(
         pack_kernel,
         (me, *in_hbm(*earlier, owner, slot)),
@@ -419,22 +491,26 @@
     )
 
     block = largest(reactions, 512, 256, 128)
-    product_t, done = pl.pallas_call(
+    product_t, head, done = call(
         product_kernel,
-        grid=(reactions // block,),
-        out_shape=(
+        in_hbm(yielded_species, consumed_species, send),
+        [HBM] * 3,
+        (
             pltpu.HBM((reactions, species), bf16),
-            jax.ShapeDtypeStruct((8, 128), f32),
+            pltpu.HBM((block, species), bf16),
+            (8, 128),
         ),
-        in_specs=[pl.BlockSpec((2, block), lambda b: (0, b)), ANY],
-        out_specs=(
-            pl.BlockSpec((block, species), lambda b: (b, 0)),
-            pl.BlockSpec((8, 128), lambda b: (0, 0)),
-        ),
-        compiler_params=pltpu.CompilerParams(vmem_limit_bytes=16 * 2**20),
-        cost_estimate=table_cost(species, reactions, 1),
-    )(*in_hbm(yielded_species), send)
-
+        [
+            pltpu.VMEM((2, reactions), i32),
+            pltpu.VMEM((2, block), i32),
+            pltpu.VMEM((reactions, species), bf16),
+            pltpu.VMEM((block, species), bf16),
+            pltpu.SemaphoreType.DMA((2,)),
+            pltpu.SemaphoreType.DMA((reactions // block + 1,)),
+        ],
+        limit=24,
+        cost=table_cost(species, reactions, 1),
+    )
     recv = exchange(send)
     ready = (
         owner,
@@ -447,8 +523,8 @@
     ready_scratch, _ = like(*earlier, *ready)
     state, heat, *prepared, consumed = call(
         prepare_kernel,
-        (me, *in_hbm(*earlier, *ready, consumed_species), send),
-        [SMEM] + [HBM] * 11 + [ANY],
+        (me, *in_hbm(*earlier, *ready, consumed_species, send)),
+        [SMEM] + [HBM] * 12,
         (
             (n, species),
             (n, EXTRA),
@@ -463,7 +539,7 @@
         ),
         [*ready_scratch, pltpu.SemaphoreType.DMA((11,))],
     )
-    flow, heat, to_inner, to_outer, place = call(
+    flow, heat, to_outer, to_inner, place = call(
         flow_kernel,
         (me, recv, state, heat, done),
         [SMEM] + [VMEM] * 3 + [ANY],
@@ -475,14 +551,14 @@
     from_inner = lax.ppermute(to_inner, "cells", inner)
     tables = call(
         react_kernel,
-        (consumed, *in_hbm(product_t), heat),
-        [VMEM, HBM, ANY],
+        (consumed, *in_hbm(product_t, head), heat),
+        [VMEM, HBM, HBM, ANY],
         (
             jax.ShapeDtypeStruct((species, reactions), bf16),
             jax.ShapeDtypeStruct((reactions, species), bf16),
             jax.ShapeDtypeStruct((reactions, species), bf16),
         ),
-        [pltpu.SemaphoreType.DMA((1,))],
+        [pltpu.SemaphoreType.DMA((2,))],
         limit=4,
         cost=table_cost(species, reactions, 2),
     )
@@ -490,13 +566,37 @@
         chemistry_kernel,
         (me, flow, heat, from_inner, from_outer, *tables, *prepared),
         [SMEM] + [VMEM] * (7 + len(prepared)),
-        ((n, species), (n, species), (partners, CAP, species)),
-        [pltpu.VMEM((n, reactions), bf16), pltpu.VMEM((n, species), bf16)],
+        (
+            pltpu.HBM((n, species), f32),
+            (n, species),
+            pltpu.HBM((partners, CAP, species), f32),
+        ),
+        [
+            pltpu.VMEM((n, reactions), bf16),
+            pltpu.VMEM((n, species), bf16),
+            pltpu.VMEM((n, species), f32),
+            pltpu.SemaphoreType.DMA((len(parts) + 1,)),
+            *parts_scratch,
+        ],
         limit=6,
     )
     recv = exchange(send)
-    (stay,) = call(stay_kernel, (me, chem, owner, slot), [SMEM] + [VMEM] * 3, ((n, species),))
-    (chem_next,) = call(land_kernel, (recv, place, stay), [VMEM] * 3, ((n, species),))
+    stay, land = call(
+        stay_kernel,
+        (me, chem, place, owner, slot),
+        [SMEM] + [VMEM] * 4,
+        ((n, species), (n, partners * CAP)),
+    )
+    (chem_next,) = call(
+        land_kernel,
+        (recv, land, stay),
+        [VMEM] * 3,
+        (pltpu.HBM((n, species), f32),),
+        [
+            pltpu.SemaphoreType.DMA((len(parts),)),
+            *[pltpu.VMEM((n, species // len(parts)), f32) for _ in parts],
+        ],
+    )
     return (spread, chem_next)
 
 

time: 66 us -> 64.3 us (0.974)
  Pallas kernels: 36.4 us -> 32.5 us
  waiting for transfers between devices: 15.6 us -> 17.6 us
    pallas_call x1 -> x0, Pallas kernels: 8.93 us -> none  [local(): pl.pallas_call(product_kernel, grid=(reactions // block,), out_shape=(plt...]
    pallas_call x7 -> x8, Pallas kernels: 27.4 us -> 32.5 us  [call(): pl.pallas_call(kernel, out_shape=outputs, in_specs=specs, out_specs=tuple...]
    all_to_all x2, waiting for transfers between devices: 15.6 us -> 17.6 us  [exchange(): return lax.all_to_all(x, 'cells', split_axis=0, concat_axis=0, tiled=True)]
  transfers between devices with their start and end apart: 4 -> 4, of which waited for: 2 -> 2; matrix products, arithmetic and copies ran while one was open for 0% -> 0% of each run, Pallas kernels for 28% -> 25%
where the time goes in v3:
time: 64.3 us; the launch traced here: 64 us
  Pallas kernels  32.5 us (51%)
  waiting for transfers between devices  17.6 us (27%)
  starting transfers between devices  12.9 us (20%)
  between operations  0.93 us (1%)
    pallas_call x8, Pallas kernels, call(): pl.pallas_call(kernel, out_shape=outputs, in_specs=specs, out_specs=tuple...  32.5 us
    all_to_all x2, waiting for transfers between devices, exchange(): return lax.all_to_all(x, 'cells', split_axis=0, concat_axis=0, tiled=True)  17.6 us
    all_to_all x2, starting transfers between devices, exchange(): return lax.all_to_all(x, 'cells', split_axis=0, concat_axis=0, tiled=True)  12.1 us
  transfers between devices with their start and end apart: 4, of which 2 were waited for; matrix products, arithmetic and copies ran while one was open for 0% of the time, Pallas kernels for 25%

profile of v3, /device:TPU:0, one launch (start us, length us, event | category | flops | bytes accessed | tf_op | source)
XLA Modules:
  0.0 64.0 jit_solution(6137494738241025628)
XLA Ops:
  0.6 2.3 %shard_map.140.after_ref.after_hbm = f32[32,2,1664]{2,1,0:T(2,128)} custom-call(s32[1]{0:T(128)} %bitcast.me_ref, f32[128,1536]{1,0:T(8,128)} %rows_hbm.3, f32[1,128]{1,0:T(1,128)} %bitcast.17, s32[1,128]{1,0:T(1,128)} %bitcast.19, s32[1,128]{1,0:T(1,128)} %bitcast.21, s32[1,128]{1,0:T(1,128)} %bitcast.9, s32[1,128]{1,0:T(1,128)} %bitcast.12), custom_call_target="tpu_custom_call" | custom-call | tf_op jit(solution)/shard_map/pallas_call | solution.py:428
  3.0 7.3 %all-to-all-start = ((f32[32,2,1664]{2,1,0:T(2,128)}), f32[32,2,1664]{2,1,0:T(2,128)S(1)}, u32[]{:S(2)}, u32[]{:S(2)}) async-start(f32[32,2,1664]{2,1,0:T(2,128)} %shard_map.140.after_ref.after_hbm), calls=%async_computation | async-start | bytes 851968 | tf_op jit(solution)/shard_map/all_to_all | solution.py:473
  10.3 1.8 %shard_map.141 = (f32[128,1536]{1,0:T(8,128)S(1)}, f32[128,128]{1,0:T(8,128)S(1)}, f32[64,128]{1,0:T(8,128)S(1)}, bf16[192,128]{1,0:T(8,128)(2,1)S(1)}, bf16[192...) custom-call(s32[1]{0:T(128)} %bitcast.me_ref, ...), custom_call_target="tpu_custom_call" | custom-call | tf_op jit(solution)/shard_map/pallas_call | solution.py:428
  12.1 7.1 %shard_map.142 = (bf16[4608,1536]{1,0:T(8,128)(2,1)}, bf16[512,1536]{1,0:T(8,128)(2,1)}, f32[8,128]{1,0:T(8,128)S(1)}) custom-call(s32[2,4608]{1,0:T(2,128)} %yielded_hbm.1, s32[2,4608]{1,0:T(2,128)} %consumed_hbm.3, f32[32,2,1664]{2,1,0:T(2,128)} %shard_map.140.after_ref.after_hbm), custom_call_target="tpu_custom_call" | custom-call | flops 283115520 | bytes 14155776 | tf_op jit(solution)/shard_map/pallas_call | solution.py:428
  19.2 4.8 %all-to-all-done.recv_ref = f32[32,2,1664]{2,1,0:T(2,128)S(1)} async-done(((f32[32,2,1664]{2,1,0:T(2,128)}), f32[32,2,1664]{2,1,0:T(2,128)S(1)}, u32[]{:S(2)}, u32[]{:S(2)}) %all-to-all-start) | async-done | bytes 426016 | tf_op jit(solution)/shard_map/all_to_all | solution.py:473
  24.0 0.5 shard_map.143
  24.6 0.1 collective-permute-start
  24.7 0.7 %collective-permute-start.1 = (f32[32,1536]{1,0:T(8,128)S(1)}, f32[32,1536]{1,0:T(8,128)S(1)}, u32[]{:S(2)}, u32[]{:S(2)}) collective-permute-start(f32[32,1536]{1,0:T(8,128)S(1)} %get-tuple-element.34), channel_id=1, source_target_pairs={{1,2},{2,1},{3,4},{4,3},{5,6},{6,5},{7,8},{8,7},{9,10},{10,9},{11,... | collective-permute-start | bytes 589832 | tf_op jit(solution)/shard_map/ppermute | solution.py:550
  25.3 6.4 %shard_map.144 = (bf16[1536,4608]{1,0:T(8,128)(2,1)S(1)}, bf16[4608,1536]{1,0:T(8,128)(2,1)S(1)}, bf16[4608,1536]{1,0:T(8,128)(2,1)S(1)}) custom-call(s32[2,4608]{1,0:T(2,128)S(1)} %get-tuple-element.35.consumed_ref, bf16[4608,1536]{1,0:T(8,128)(2,1)} %get-tuple-element.36.product_t_hbm, bf16[512,1536]{1,0:T(8,128)(2,1)} %get-tuple-element.37.head_hbm, ...), custom_call_target="tpu_custom_call" | custom-call | flops 566231040 | bytes 28311552 | tf_op jit(solution)/shard_map/pallas_call | solution.py:428
  31.7 0.0 collective-permute-done.inner_ref
  31.7 0.0 collective-permute-done.1.outer_ref
  31.8 0.0 copy-start
  31.8 0.0 copy-start.1
  31.8 12.8 %shard_map.145 = (f32[128,1536]{1,0:T(8,128)}, f32[128,1536]{1,0:T(8,128)S(1)}, f32[32,2,1536]{2,1,0:T(2,128)}) custom-call(s32[1]{0:T(128)} %bitcast.me_ref, f32[128,1536]{1,0:T(8,128)S(1)} %get-tuple-element.31.flow_ref, f32[128,128]{1,0:T(8,128)S(1)} %get-tuple-element.32.after_ref.heat_ref, f32[32,1536]{1,0:T(8,128)S(1)} %collective-permute-done.inner_ref, ...), custom_call_target="tpu_custom_call" | custom-call | tf_op jit(solution)/shard_map/pallas_call | solution.py:428
  44.5 4.8 %all-to-all-start.1 = ((f32[32,2,1536]{2,1,0:T(2,128)}), f32[32,2,1536]{2,1,0:T(2,128)S(1)}, u32[]{:S(2)}, u32[]{:S(2)}) async-start(f32[32,2,1536]{2,1,0:T(2,128)} %get-tuple-element.49), calls=%async_computation.1 | async-start | bytes 786432 | tf_op jit(solution)/shard_map/all_to_all | solution.py:473
  49.4 0.0 copy-done
  49.4 0.0 copy-done.1
  49.4 0.4 shard_map.146
  49.8 12.8 %all-to-all-done.1.recv_ref = f32[32,2,1536]{2,1,0:T(2,128)S(1)} async-done(((f32[32,2,1536]{2,1,0:T(2,128)}), f32[32,2,1536]{2,1,0:T(2,128)S(1)}, u32[]{:S(2)}, u32[]{:S(2)}) %all-to-all-start.1) | async-done | bytes 393248 | tf_op jit(solution)/shard_map/all_to_all | solution.py:473
  62.6 1.2 %shard_map.147 = f32[128,1536]{1,0:T(8,128)} custom-call(f32[32,2,1536]{2,1,0:T(2,128)S(1)} %all-to-all-done.1.recv_ref, f32[128,64]{1,0:T(8,128)S(1)} %get-tuple-element.52.land_ref, f32[128,1536]{1,0:T(8,128)S(1)} %get-tuple-element.53.stay_ref), custom_call_target="tpu_custom_call" | custom-call | tf_op jit(solution)/shard_map/pallas_call | solution.py:428
Async XLA Ops:
  3.0 21.1 %all-to-all-start = ((f32[32,2,1664]{2,1,0:T(2,128)}), f32[32,2,1664]{2,1,0:T(2,128)S(1)}, u32[]{:S(2)}, u32[]{:S(2)}) async-start(f32[32,2,1664]{2,1,0:T(2,128)} %shard_map.140.after_ref.after_hbm), calls=%async_computation | async-start | bytes 851968 | tf_op jit(solution)/shard_map/all_to_all | solution.py:473
  24.6 7.2 %collective-permute-start = (f32[32,1536]{1,0:T(8,128)S(1)}, f32[32,1536]{1,0:T(8,128)S(1)}, u32[]{:S(2)}, u32[]{:S(2)}) collective-permute-start(f32[32,1536]{1,0:T(8,128)S(1)} %get-tuple-element.33), channel_id=1, source_target_pairs={{0,1},{1,0},{2,3},{3,2},{4,5},{5,4},{6,7},{7,6},{8,9},{9,8},{10,11... | collective-permute-start | bytes 589832 | tf_op jit(solution)/shard_map/ppermute | solution.py:551
  24.7 7.1 %collective-permute-start.1 = (f32[32,1536]{1,0:T(8,128)S(1)}, f32[32,1536]{1,0:T(8,128)S(1)}, u32[]{:S(2)}, u32[]{:S(2)}) collective-permute-start(f32[32,1536]{1,0:T(8,128)S(1)} %get-tuple-element.34), channel_id=1, source_target_pairs={{1,2},{2,1},{3,4},{4,3},{5,6},{6,5},{7,8},{8,7},{9,10},{10,9},{11,... | collective-permute-start | bytes 589832 | tf_op jit(solution)/shard_map/ppermute | solution.py:550
  31.8 17.6 %copy-start = (s32[128]{0:T(128)S(1)}, s32[128]{0:T(128)}, u32[]{:S(2)}) copy-start(s32[128]{0:T(128)} %param.20) | copy-start | bytes 1540
  31.8 17.6 %copy-start.1 = (s32[128]{0:T(128)S(1)}, s32[128]{0:T(128)}, u32[]{:S(2)}) copy-start(s32[128]{0:T(128)} %param.21) | copy-start | bytes 1540
  44.5 18.0 %all-to-all-start.1 = ((f32[32,2,1536]{2,1,0:T(2,128)}), f32[32,2,1536]{2,1,0:T(2,128)S(1)}, u32[]{:S(2)}, u32[]{:S(2)}) async-start(f32[32,2,1536]{2,1,0:T(2,128)} %get-tuple-element.49), calls=%async_computation.1 | async-start | bytes 786432 | tf_op jit(solution)/shard_map/all_to_all | solution.py:473

commit v4 on v3

--- a/solution.py
+++ b/solution.py
@@ -76,8 +76,8 @@
     return copies
 
 
-def pieces(total):
-    width = largest(total, 768, 512, 256, 128)
+def pieces(total, *widths):
+    width = largest(total, *widths, 256, 128)
     return [slice(first, first + width) for first in range(0, total, width)]
 
 
@@ -279,9 +279,11 @@
     sems,
     out_sems,
 ):
-    block, species = head.shape
-    blocks = product_t.shape[0] // block
-    finish(begin((yielded_hbm, consumed_hbm.at[:, :block]), (yielded, consumed), sems))
+    reactions, species = product_t.shape
+    block = largest(reactions, 512, 256, 128)
+    blocks = reactions // block
+    many = head.shape[0]
+    finish(begin((yielded_hbm, consumed_hbm.at[:, :many]), (yielded, consumed), sems))
 
     def out(b):
         at = pl.ds(pl.multiple_of(b * block, block), block)
@@ -300,7 +302,9 @@
         return carry
 
     lax.fori_loop(0, blocks, fill, 0, unroll=largest(blocks, 3, 2, 1))
-    head[...] = column_table(consumed[...])(species)
+    for first in range(0, many, block):
+        at = slice(first, first + block)
+        head[at, :] = column_table(consumed[:, at])(species)
     left = leave(head, head_hbm, out_sems.at[blocks])
     done_ref[...] = jnp.zeros_like(done_ref)
     lax.fori_loop(0, blocks, drain, 0)
@@ -317,10 +321,11 @@
     product_t_ref,
     sems,
 ):
-    block = head_hbm.shape[0]
-    targets = (product_t_ref, react_t_ref.at[:block, :])
+    many = head_hbm.shape[0]
+    targets = (product_t_ref, react_t_ref.at[:many, :])
     copies = begin((product_t_hbm, head_hbm), targets, sems)
     species, reactions = react_ref.shape
+    block = largest(reactions, 512, 256, 128)
     down_species = iota((species, block), 0).astype(i16)
 
     def fill(b, carry):
@@ -335,8 +340,10 @@
         return carry
 
     lax.fori_loop(0, reactions // block, fill, 0)
-    rest = reactions // block - 1
-    lax.fori_loop(1, rest + 1, fill_t, 0, unroll=largest(rest, 4, 3, 2, 1))
+    blocks = reactions // block
+    odd = many // block + (blocks - many // block) % 3
+    lax.fori_loop(many // block, odd, fill_t, 0)
+    lax.fori_loop(odd, blocks, fill_t, 0, unroll=3)
     finish(copies)
 
 
@@ -402,7 +409,7 @@
             chem_ref[:, at] = (spread_ref[:, at] + time_step * gain) / (
                 1.0 + time_step * loss / chem_ref[:, at]
             )
-    for i, at in enumerate(pieces(species)):
+    for i, at in enumerate(pieces(species, 768, 512)):
         out[i][...] = pick(choice_ref[...], chem_ref[:, at]).reshape(out[i].shape)
         left.append(leave(out[i], send_hbm.at[:, :, at], out_sems.at[i]))
     finish(left)
@@ -416,7 +423,7 @@
 def land_kernel(recv_ref, land_ref, stay_ref, out_hbm, out_sems, *out):
     partners, cap, species = recv_ref.shape
     left = []
-    for i, at in enumerate(pieces(species)):
+    for i, at in enumerate(pieces(species, 384)):
         got = recv_ref[:, :, at].reshape(partners * cap, -1)
         out[i][...] = pick(land_ref[...], got) + stay_ref[:, at]
         left.append(leave(out[i], out_hbm.at[:, at], out_sems.at[i]))
@@ -480,7 +487,7 @@
     )
     owner, slot = row(present_kinetics_holder), row(present_kinetics_slot)
     pack_scratch, pack_sems = like(*earlier, owner, slot)
-    parts = pieces(species)
+    parts = pieces(species, 768, 512)
     parts_scratch = [pltpu.VMEM((partners, CAP, species // len(parts)), f32) for _ in parts]
     (send,) = call(
         pack_kernel,
@@ -497,14 +504,14 @@
         [HBM] * 3,
         (
             pltpu.HBM((reactions, species), bf16),
-            pltpu.HBM((block, species), bf16),
+            pltpu.HBM((2 * block, species), bf16),
             (8, 128),
         ),
         [
             pltpu.VMEM((2, reactions), i32),
-            pltpu.VMEM((2, block), i32),
+            pltpu.VMEM((2, 2 * block), i32),
             pltpu.VMEM((reactions, species), bf16),
-            pltpu.VMEM((block, species), bf16),
+            pltpu.VMEM((2 * block, species), bf16),
             pltpu.SemaphoreType.DMA((2,)),
             pltpu.SemaphoreType.DMA((reactions // block + 1,)),
         ],
@@ -547,8 +554,8 @@
     )
     inner = [(i, i ^ 1) for i in range(partners)]
     outer = [(i, ((i + 1) ^ 1) - 1) for i in range(1, partners - 1)]
+    from_inner = lax.ppermute(to_inner, "cells", inner)
     from_outer = lax.ppermute(to_outer, "cells", outer)
-    from_inner = lax.ppermute(to_inner, "cells", inner)
     tables = call(
         react_kernel,
         (consumed, *in_hbm(product_t, head), heat),
@@ -587,14 +594,15 @@
         [SMEM] + [VMEM] * 4,
         ((n, species), (n, partners * CAP)),
     )
+    ends = pieces(species, 384)
     (chem_next,) = call(
         land_kernel,
         (recv, land, stay),
         [VMEM] * 3,
         (pltpu.HBM((n, species), f32),),
         [
-            pltpu.SemaphoreType.DMA((len(parts),)),
-            *[pltpu.VMEM((n, species // len(parts)), f32) for _ in parts],
+            pltpu.SemaphoreType.DMA((len(ends),)),
+            *[pltpu.VMEM((n, species // len(ends)), f32) for _ in ends],
         ],
     )
     return (spread, chem_next)

time: 64.3 us -> 64 us (level)
  no operation moved by 1% of the time
where the time goes in v4:
time: 64 us; the launch traced here: 63.6 us
  Pallas kernels  32.6 us (51%)
  waiting for transfers between devices  17.2 us (27%)
  starting transfers between devices  12.9 us (20%)
  between operations  0.93 us (1%)
    pallas_call x8, Pallas kernels, call(): pl.pallas_call(kernel, out_shape=outputs, in_specs=specs, out_specs=tuple...  32.6 us
    all_to_all x2, waiting for transfers between devices, exchange(): return lax.all_to_all(x, 'cells', split_axis=0, concat_axis=0, tiled=True)  17.2 us
    all_to_all x2, starting transfers between devices, exchange(): return lax.all_to_all(x, 'cells', split_axis=0, concat_axis=0, tiled=True)  12.1 us
  transfers between devices with their start and end apart: 4, of which 2 were waited for; matrix products, arithmetic and copies ran while one was open for 0% of the time, Pallas kernels for 25%

profile of v4, /device:TPU:0, one launch (start us, length us, event | category | flops | bytes accessed | tf_op | source)
XLA Modules:
  0.0 63.6 jit_solution(15833553873715496297)
XLA Ops:
  0.6 2.3 %shard_map.140.after_ref.after_hbm = f32[32,2,1664]{2,1,0:T(2,128)} custom-call(s32[1]{0:T(128)} %bitcast.me_ref, f32[128,1536]{1,0:T(8,128)} %rows_hbm.3, f32[1,128]{1,0:T(1,128)} %bitcast.17, s32[1,128]{1,0:T(1,128)} %bitcast.19, s32[1,128]{1,0:T(1,128)} %bitcast.21, s32[1,128]{1,0:T(1,128)} %bitcast.9, s32[1,128]{1,0:T(1,128)} %bitcast.12), custom_call_target="tpu_custom_call" | custom-call | tf_op jit(solution)/shard_map/pallas_call | solution.py:435
  3.0 7.3 %all-to-all-start = ((f32[32,2,1664]{2,1,0:T(2,128)}), f32[32,2,1664]{2,1,0:T(2,128)S(1)}, u32[]{:S(2)}, u32[]{:S(2)}) async-start(f32[32,2,1664]{2,1,0:T(2,128)} %shard_map.140.after_ref.after_hbm), calls=%async_computation | async-start | bytes 851968 | tf_op jit(solution)/shard_map/all_to_all | solution.py:480
  10.3 1.8 %shard_map.141 = (f32[128,1536]{1,0:T(8,128)S(1)}, f32[128,128]{1,0:T(8,128)S(1)}, f32[64,128]{1,0:T(8,128)S(1)}, bf16[192,128]{1,0:T(8,128)(2,1)S(1)}, bf16[192...) custom-call(s32[1]{0:T(128)} %bitcast.me_ref, ...), custom_call_target="tpu_custom_call" | custom-call | tf_op jit(solution)/shard_map/pallas_call | solution.py:435
  12.1 7.5 %shard_map.142 = (bf16[4608,1536]{1,0:T(8,128)(2,1)}, bf16[1024,1536]{1,0:T(8,128)(2,1)}, f32[8,128]{1,0:T(8,128)S(1)}) custom-call(s32[2,4608]{1,0:T(2,128)} %yielded_hbm.1, s32[2,4608]{1,0:T(2,128)} %consumed_hbm.3, f32[32,2,1664]{2,1,0:T(2,128)} %shard_map.140.after_ref.after_hbm), custom_call_target="tpu_custom_call" | custom-call | flops 283115520 | bytes 14155776 | tf_op jit(solution)/shard_map/pallas_call | solution.py:435
  19.6 4.4 %all-to-all-done.recv_ref = f32[32,2,1664]{2,1,0:T(2,128)S(1)} async-done(((f32[32,2,1664]{2,1,0:T(2,128)}), f32[32,2,1664]{2,1,0:T(2,128)S(1)}, u32[]{:S(2)}, u32[]{:S(2)}) %all-to-all-start) | async-done | bytes 426016 | tf_op jit(solution)/shard_map/all_to_all | solution.py:480
  24.0 0.5 shard_map.143
  24.6 0.1 collective-permute-start
  24.7 0.7 %collective-permute-start.1 = (f32[32,1536]{1,0:T(8,128)S(1)}, f32[32,1536]{1,0:T(8,128)S(1)}, u32[]{:S(2)}, u32[]{:S(2)}) collective-permute-start(f32[32,1536]{1,0:T(8,128)S(1)} %get-tuple-element.34), channel_id=1, source_target_pairs={{1,2},{2,1},{3,4},{4,3},{5,6},{6,5},{7,8},{8,7},{9,10},{10,9},{11,... | collective-permute-start | bytes 589832 | tf_op jit(solution)/shard_map/ppermute | solution.py:558
  25.3 6.1 %shard_map.144 = (bf16[1536,4608]{1,0:T(8,128)(2,1)S(1)}, bf16[4608,1536]{1,0:T(8,128)(2,1)S(1)}, bf16[4608,1536]{1,0:T(8,128)(2,1)S(1)}) custom-call(s32[2,4608]{1,0:T(2,128)S(1)} %get-tuple-element.35.consumed_ref, bf16[4608,1536]{1,0:T(8,128)(2,1)} %get-tuple-element.36.product_t_hbm, bf16[1024,1536]{1,0:T(8,128)(2,1)} %get-tuple-element.37.head_hbm, ...), custom_call_target="tpu_custom_call" | custom-call | flops 566231040 | bytes 28311552 | tf_op jit(solution)/shard_map/pallas_call | solution.py:435
  31.4 0.0 collective-permute-done.inner_ref
  31.4 0.0 collective-permute-done.1.outer_ref
  31.4 0.0 copy-start
  31.5 0.0 copy-start.1
  31.5 12.8 %shard_map.145 = (f32[128,1536]{1,0:T(8,128)}, f32[128,1536]{1,0:T(8,128)S(1)}, f32[32,2,1536]{2,1,0:T(2,128)}) custom-call(s32[1]{0:T(128)} %bitcast.me_ref, f32[128,1536]{1,0:T(8,128)S(1)} %get-tuple-element.31.flow_ref, f32[128,128]{1,0:T(8,128)S(1)} %get-tuple-element.32.after_ref.heat_ref, f32[32,1536]{1,0:T(8,128)S(1)} %collective-permute-done.inner_ref, ...), custom_call_target="tpu_custom_call" | custom-call | tf_op jit(solution)/shard_map/pallas_call | solution.py:435
  44.2 4.8 %all-to-all-start.1 = ((f32[32,2,1536]{2,1,0:T(2,128)}), f32[32,2,1536]{2,1,0:T(2,128)S(1)}, u32[]{:S(2)}, u32[]{:S(2)}) async-start(f32[32,2,1536]{2,1,0:T(2,128)} %get-tuple-element.49), calls=%async_computation.1 | async-start | bytes 786432 | tf_op jit(solution)/shard_map/all_to_all | solution.py:480
  49.1 0.0 copy-done
  49.1 0.0 copy-done.1
  49.1 0.4 shard_map.146
  49.5 12.8 %all-to-all-done.1.recv_ref = f32[32,2,1536]{2,1,0:T(2,128)S(1)} async-done(((f32[32,2,1536]{2,1,0:T(2,128)}), f32[32,2,1536]{2,1,0:T(2,128)S(1)}, u32[]{:S(2)}, u32[]{:S(2)}) %all-to-all-start.1) | async-done | bytes 393248 | tf_op jit(solution)/shard_map/all_to_all | solution.py:480
  62.3 1.2 %shard_map.147 = f32[128,1536]{1,0:T(8,128)} custom-call(f32[32,2,1536]{2,1,0:T(2,128)S(1)} %all-to-all-done.1.recv_ref, f32[128,64]{1,0:T(8,128)S(1)} %get-tuple-element.52.land_ref, f32[128,1536]{1,0:T(8,128)S(1)} %get-tuple-element.53.stay_ref), custom_call_target="tpu_custom_call" | custom-call | tf_op jit(solution)/shard_map/pallas_call | solution.py:435
Async XLA Ops:
  3.0 21.1 %all-to-all-start = ((f32[32,2,1664]{2,1,0:T(2,128)}), f32[32,2,1664]{2,1,0:T(2,128)S(1)}, u32[]{:S(2)}, u32[]{:S(2)}) async-start(f32[32,2,1664]{2,1,0:T(2,128)} %shard_map.140.after_ref.after_hbm), calls=%async_computation | async-start | bytes 851968 | tf_op jit(solution)/shard_map/all_to_all | solution.py:480
  24.6 6.9 %collective-permute-start = (f32[32,1536]{1,0:T(8,128)S(1)}, f32[32,1536]{1,0:T(8,128)S(1)}, u32[]{:S(2)}, u32[]{:S(2)}) collective-permute-start(f32[32,1536]{1,0:T(8,128)S(1)} %get-tuple-element.33), channel_id=1, source_target_pairs={{0,1},{1,0},{2,3},{3,2},{4,5},{5,4},{6,7},{7,6},{8,9},{9,8},{10,11... | collective-permute-start | bytes 589832 | tf_op jit(solution)/shard_map/ppermute | solution.py:557
  24.7 6.8 %collective-permute-start.1 = (f32[32,1536]{1,0:T(8,128)S(1)}, f32[32,1536]{1,0:T(8,128)S(1)}, u32[]{:S(2)}, u32[]{:S(2)}) collective-permute-start(f32[32,1536]{1,0:T(8,128)S(1)} %get-tuple-element.34), channel_id=1, source_target_pairs={{1,2},{2,1},{3,4},{4,3},{5,6},{6,5},{7,8},{8,7},{9,10},{10,9},{11,... | collective-permute-start | bytes 589832 | tf_op jit(solution)/shard_map/ppermute | solution.py:558
  31.4 17.6 %copy-start = (s32[128]{0:T(128)S(1)}, s32[128]{0:T(128)}, u32[]{:S(2)}) copy-start(s32[128]{0:T(128)} %param.20) | copy-start | bytes 1540
  31.5 17.6 %copy-start.1 = (s32[128]{0:T(128)S(1)}, s32[128]{0:T(128)}, u32[]{:S(2)}) copy-start(s32[128]{0:T(128)} %param.21) | copy-start | bytes 1540
  44.2 18.0 %all-to-all-start.1 = ((f32[32,2,1536]{2,1,0:T(2,128)}), f32[32,2,1536]{2,1,0:T(2,128)S(1)}, u32[]{:S(2)}, u32[]{:S(2)}) async-start(f32[32,2,1536]{2,1,0:T(2,128)} %get-tuple-element.49), calls=%async_computation.1 | async-start | bytes 786432 | tf_op jit(solution)/shard_map/all_to_all | solution.py:480

commit v5 on v4

--- a/solution.py
+++ b/solution.py
@@ -76,8 +76,8 @@
     return copies
 
 
-def pieces(total, *widths):
-    width = largest(total, *widths, 256, 128)
+def folds(total):
+    width = total // 4 if total % 512 == 0 else total
     return [slice(first, first + width) for first in range(0, total, width)]
 
 
@@ -409,9 +409,10 @@
             chem_ref[:, at] = (spread_ref[:, at] + time_step * gain) / (
                 1.0 + time_step * loss / chem_ref[:, at]
             )
-    for i, at in enumerate(pieces(species, 768, 512)):
-        out[i][...] = pick(choice_ref[...], chem_ref[:, at]).reshape(out[i].shape)
-        left.append(leave(out[i], send_hbm.at[:, :, at], out_sems.at[i]))
+    for j, at in enumerate(folds(species)):
+        moved = pick(choice_ref[...], chem_ref[:, at])
+        out[0][:, j * CAP : (j + 1) * CAP, :] = moved.reshape(-1, CAP, moved.shape[1])
+    left.append(leave(out[0], send_hbm, out_sems.at[0]))
     finish(left)
 
 
@@ -421,12 +422,13 @@
 
 
 def land_kernel(recv_ref, land_ref, stay_ref, out_hbm, out_sems, *out):
-    partners, cap, species = recv_ref.shape
+    partners, _, width = recv_ref.shape
+    species = out_hbm.shape[1]
     left = []
-    for i, at in enumerate(pieces(species, 384)):
-        got = recv_ref[:, :, at].reshape(partners * cap, -1)
-        out[i][...] = pick(land_ref[...], got) + stay_ref[:, at]
-        left.append(leave(out[i], out_hbm.at[:, at], out_sems.at[i]))
+    for j, at in enumerate(folds(species)):
+        got = recv_ref[:, j * CAP : (j + 1) * CAP, :].reshape(partners * CAP, width)
+        out[j][...] = pick(land_ref[...], got) + stay_ref[:, at]
+        left.append(leave(out[j], out_hbm.at[:, at], out_sems.at[j]))
     finish(left)
 
 
@@ -487,8 +489,8 @@
     )
     owner, slot = row(present_kinetics_holder), row(present_kinetics_slot)
     pack_scratch, pack_sems = like(*earlier, owner, slot)
-    parts = pieces(species, 768, 512)
-    parts_scratch = [pltpu.VMEM((partners, CAP, species // len(parts)), f32) for _ in parts]
+    ends = folds(species)
+    folded = (partners, CAP * len(ends), species // len(ends))
     (send,) = call(
         pack_kernel,
         (me, *in_hbm(*earlier, owner, slot)),
@@ -576,14 +578,14 @@
         (
             pltpu.HBM((n, species), f32),
             (n, species),
-            pltpu.HBM((partners, CAP, species), f32),
+            pltpu.HBM(folded, f32),
         ),
         [
             pltpu.VMEM((n, reactions), bf16),
             pltpu.VMEM((n, species), bf16),
             pltpu.VMEM((n, species), f32),
-            pltpu.SemaphoreType.DMA((len(parts) + 1,)),
-            *parts_scratch,
+            pltpu.SemaphoreType.DMA((2,)),
+            pltpu.VMEM(folded, f32),
         ],
         limit=6,
     )
@@ -594,7 +596,6 @@
         [SMEM] + [VMEM] * 4,
         ((n, species), (n, partners * CAP)),
     )
-    ends = pieces(species, 384)
     (chem_next,) = call(
         land_kernel,
         (recv, land, stay),

time: 64 us -> 64 us (level)
  no operation moved by 1% of the time
where the time goes in v5:
time: 64 us; the launch traced here: 63.6 us
  Pallas kernels  32.6 us (51%)
  waiting for transfers between devices  17.2 us (27%)
  starting transfers between devices  12.9 us (20%)
  between operations  0.93 us (1%)
    pallas_call x8, Pallas kernels, call(): pl.pallas_call(kernel, out_shape=outputs, in_specs=specs, out_specs=tuple...  32.6 us
    all_to_all x2, waiting for transfers between devices, exchange(): return lax.all_to_all(x, 'cells', split_axis=0, concat_axis=0, tiled=True)  17.2 us
    all_to_all x2, starting transfers between devices, exchange(): return lax.all_to_all(x, 'cells', split_axis=0, concat_axis=0, tiled=True)  12.1 us
  transfers between devices with their start and end apart: 4, of which 2 were waited for; matrix products, arithmetic and copies ran while one was open for 0% of the time, Pallas kernels for 25%

profile of v5, /device:TPU:0, one launch (start us, length us, event | category | flops | bytes accessed | tf_op | source)
XLA Modules:
  0.0 63.6 jit_solution(11036597566249396774)
XLA Ops:
  0.6 2.3 %shard_map.140.after_ref.after_hbm = f32[32,2,1664]{2,1,0:T(2,128)} custom-call(s32[1]{0:T(128)} %bitcast.me_ref, f32[128,1536]{1,0:T(8,128)} %rows_hbm.3, f32[1,128]{1,0:T(1,128)} %bitcast.17, s32[1,128]{1,0:T(1,128)} %bitcast.19, s32[1,128]{1,0:T(1,128)} %bitcast.21, s32[1,128]{1,0:T(1,128)} %bitcast.9, s32[1,128]{1,0:T(1,128)} %bitcast.12), custom_call_target="tpu_custom_call" | custom-call | tf_op jit(solution)/shard_map/pallas_call | solution.py:437
  3.0 7.3 %all-to-all-start = ((f32[32,2,1664]{2,1,0:T(2,128)}), f32[32,2,1664]{2,1,0:T(2,128)S(1)}, u32[]{:S(2)}, u32[]{:S(2)}) async-start(f32[32,2,1664]{2,1,0:T(2,128)} %shard_map.140.after_ref.after_hbm), calls=%async_computation | async-start | bytes 851968 | tf_op jit(solution)/shard_map/all_to_all | solution.py:482
  10.3 1.8 %shard_map.141 = (f32[128,1536]{1,0:T(8,128)S(1)}, f32[128,128]{1,0:T(8,128)S(1)}, f32[64,128]{1,0:T(8,128)S(1)}, bf16[192,128]{1,0:T(8,128)(2,1)S(1)}, bf16[192...) custom-call(s32[1]{0:T(128)} %bitcast.me_ref, ...), custom_call_target="tpu_custom_call" | custom-call | tf_op jit(solution)/shard_map/pallas_call | solution.py:437
  12.1 7.5 %shard_map.142 = (bf16[4608,1536]{1,0:T(8,128)(2,1)}, bf16[1024,1536]{1,0:T(8,128)(2,1)}, f32[8,128]{1,0:T(8,128)S(1)}) custom-call(s32[2,4608]{1,0:T(2,128)} %yielded_hbm.1, s32[2,4608]{1,0:T(2,128)} %consumed_hbm.3, f32[32,2,1664]{2,1,0:T(2,128)} %shard_map.140.after_ref.after_hbm), custom_call_target="tpu_custom_call" | custom-call | flops 283115520 | bytes 14155776 | tf_op jit(solution)/shard_map/pallas_call | solution.py:437
  19.6 4.4 %all-to-all-done.recv_ref = f32[32,2,1664]{2,1,0:T(2,128)S(1)} async-done(((f32[32,2,1664]{2,1,0:T(2,128)}), f32[32,2,1664]{2,1,0:T(2,128)S(1)}, u32[]{:S(2)}, u32[]{:S(2)}) %all-to-all-start) | async-done | bytes 426016 | tf_op jit(solution)/shard_map/all_to_all | solution.py:482
  24.0 0.5 shard_map.143
  24.6 0.1 collective-permute-start
  24.7 0.7 %collective-permute-start.1 = (f32[32,1536]{1,0:T(8,128)S(1)}, f32[32,1536]{1,0:T(8,128)S(1)}, u32[]{:S(2)}, u32[]{:S(2)}) collective-permute-start(f32[32,1536]{1,0:T(8,128)S(1)} %get-tuple-element.34), channel_id=1, source_target_pairs={{1,2},{2,1},{3,4},{4,3},{5,6},{6,5},{7,8},{8,7},{9,10},{10,9},{11,... | collective-permute-start | bytes 589832 | tf_op jit(solution)/shard_map/ppermute | solution.py:560
  25.3 6.1 %shard_map.144 = (bf16[1536,4608]{1,0:T(8,128)(2,1)S(1)}, bf16[4608,1536]{1,0:T(8,128)(2,1)S(1)}, bf16[4608,1536]{1,0:T(8,128)(2,1)S(1)}) custom-call(s32[2,4608]{1,0:T(2,128)S(1)} %get-tuple-element.35.consumed_ref, bf16[4608,1536]{1,0:T(8,128)(2,1)} %get-tuple-element.36.product_t_hbm, bf16[1024,1536]{1,0:T(8,128)(2,1)} %get-tuple-element.37.head_hbm, ...), custom_call_target="tpu_custom_call" | custom-call | flops 566231040 | bytes 28311552 | tf_op jit(solution)/shard_map/pallas_call | solution.py:437
  31.4 0.0 collective-permute-done.inner_ref
  31.4 0.0 collective-permute-done.1.outer_ref
  31.4 0.0 copy-start
  31.5 0.0 copy-start.1
  31.5 12.8 %shard_map.145 = (f32[128,1536]{1,0:T(8,128)}, f32[128,1536]{1,0:T(8,128)S(1)}, f32[32,8,384]{2,1,0:T(8,128)}) custom-call(s32[1]{0:T(128)} %bitcast.me_ref, f32[128,1536]{1,0:T(8,128)S(1)} %get-tuple-element.31.flow_ref, f32[128,128]{1,0:T(8,128)S(1)} %get-tuple-element.32.after_ref.heat_ref, f32[32,1536]{1,0:T(8,128)S(1)} %collective-permute-done.inner_ref, ...), custom_call_target="tpu_custom_call" | custom-call | tf_op jit(solution)/shard_map/pallas_call | solution.py:437
  44.2 4.8 %all-to-all-start.1 = ((f32[32,8,384]{2,1,0:T(8,128)}), f32[32,8,384]{2,1,0:T(8,128)S(1)}, u32[]{:S(2)}, u32[]{:S(2)}) async-start(f32[32,8,384]{2,1,0:T(8,128)} %get-tuple-element.49), calls=%async_computation.1 | async-start | bytes 786432 | tf_op jit(solution)/shard_map/all_to_all | solution.py:482
  49.1 0.0 copy-done
  49.1 0.0 copy-done.1
  49.1 0.4 shard_map.146
  49.5 12.8 %all-to-all-done.1.recv_ref = f32[32,8,384]{2,1,0:T(8,128)S(1)} async-done(((f32[32,8,384]{2,1,0:T(8,128)}), f32[32,8,384]{2,1,0:T(8,128)S(1)}, u32[]{:S(2)}, u32[]{:S(2)}) %all-to-all-start.1) | async-done | bytes 393248 | tf_op jit(solution)/shard_map/all_to_all | solution.py:482
  62.2 1.2 %shard_map.147 = f32[128,1536]{1,0:T(8,128)} custom-call(f32[32,8,384]{2,1,0:T(8,128)S(1)} %all-to-all-done.1.recv_ref, f32[128,64]{1,0:T(8,128)S(1)} %get-tuple-element.52.land_ref, f32[128,1536]{1,0:T(8,128)S(1)} %get-tuple-element.53.stay_ref), custom_call_target="tpu_custom_call" | custom-call | tf_op jit(solution)/shard_map/pallas_call | solution.py:437
Async XLA Ops:
  3.0 21.1 %all-to-all-start = ((f32[32,2,1664]{2,1,0:T(2,128)}), f32[32,2,1664]{2,1,0:T(2,128)S(1)}, u32[]{:S(2)}, u32[]{:S(2)}) async-start(f32[32,2,1664]{2,1,0:T(2,128)} %shard_map.140.after_ref.after_hbm), calls=%async_computation | async-start | bytes 851968 | tf_op jit(solution)/shard_map/all_to_all | solution.py:482
  24.6 6.9 %collective-permute-start = (f32[32,1536]{1,0:T(8,128)S(1)}, f32[32,1536]{1,0:T(8,128)S(1)}, u32[]{:S(2)}, u32[]{:S(2)}) collective-permute-start(f32[32,1536]{1,0:T(8,128)S(1)} %get-tuple-element.33), channel_id=1, source_target_pairs={{0,1},{1,0},{2,3},{3,2},{4,5},{5,4},{6,7},{7,6},{8,9},{9,8},{10,11... | collective-permute-start | bytes 589832 | tf_op jit(solution)/shard_map/ppermute | solution.py:559
  24.7 6.8 %collective-permute-start.1 = (f32[32,1536]{1,0:T(8,128)S(1)}, f32[32,1536]{1,0:T(8,128)S(1)}, u32[]{:S(2)}, u32[]{:S(2)}) collective-permute-start(f32[32,1536]{1,0:T(8,128)S(1)} %get-tuple-element.34), channel_id=1, source_target_pairs={{1,2},{2,1},{3,4},{4,3},{5,6},{6,5},{7,8},{8,7},{9,10},{10,9},{11,... | collective-permute-start | bytes 589832 | tf_op jit(solution)/shard_map/ppermute | solution.py:560
  31.4 17.6 %copy-start = (s32[128]{0:T(128)S(1)}, s32[128]{0:T(128)}, u32[]{:S(2)}) copy-start(s32[128]{0:T(128)} %param.20) | copy-start | bytes 1540
  31.5 17.6 %copy-start.1 = (s32[128]{0:T(128)S(1)}, s32[128]{0:T(128)}, u32[]{:S(2)}) copy-start(s32[128]{0:T(128)} %param.21) | copy-start | bytes 1540
  44.2 18.0 %all-to-all-start.1 = ((f32[32,8,384]{2,1,0:T(8,128)}), f32[32,8,384]{2,1,0:T(8,128)S(1)}, u32[]{:S(2)}, u32[]{:S(2)}) async-start(f32[32,8,384]{2,1,0:T(8,128)} %get-tuple-element.49), calls=%async_computation.1 | async-start | bytes 786432 | tf_op jit(solution)/shard_map/all_to_all | solution.py:482

commit v6 on v4

--- a/solution.py
+++ b/solution.py
@@ -393,7 +393,7 @@
     inverse = 1.0 / heat_ref[:, 0:1]
     species, reactions = react_ref.shape
     across = largest(reactions, 512, 256, 128)
-    down = largest(species, 512, 256, 128)
+    down = largest(species, 256, 128)
     tiles = [slice(first, first + down) for first in range(0, species, down)]
 
     for turn in range(NEWTON):

time: 64 us -> 64 us (level)
  no operation moved by 1% of the time
where the time goes in v6:
time: 64 us; the launch traced here: 63.6 us
  Pallas kernels  32.5 us (51%)
  waiting for transfers between devices  17.2 us (27%)
  starting transfers between devices  12.9 us (20%)
  between operations  0.93 us (1%)
    pallas_call x8, Pallas kernels, call(): pl.pallas_call(kernel, out_shape=outputs, in_specs=specs, out_specs=tuple...  32.5 us
    all_to_all x2, waiting for transfers between devices, exchange(): return lax.all_to_all(x, 'cells', split_axis=0, concat_axis=0, tiled=True)  17.2 us
    all_to_all x2, starting transfers between devices, exchange(): return lax.all_to_all(x, 'cells', split_axis=0, concat_axis=0, tiled=True)  12.1 us
  transfers between devices with their start and end apart: 4, of which 2 were waited for; matrix products, arithmetic and copies ran while one was open for 0% of the time, Pallas kernels for 25%

profile of v6, /device:TPU:0, one launch (start us, length us, event | category | flops | bytes accessed | tf_op | source)
XLA Modules:
  0.0 63.6 jit_solution(2584339609639176322)
XLA Ops:
  0.6 2.3 %shard_map.140.after_ref.after_hbm = f32[32,2,1664]{2,1,0:T(2,128)} custom-call(s32[1]{0:T(128)} %bitcast.me_ref, f32[128,1536]{1,0:T(8,128)} %rows_hbm.3, f32[1,128]{1,0:T(1,128)} %bitcast.17, s32[1,128]{1,0:T(1,128)} %bitcast.19, s32[1,128]{1,0:T(1,128)} %bitcast.21, s32[1,128]{1,0:T(1,128)} %bitcast.9, s32[1,128]{1,0:T(1,128)} %bitcast.12), custom_call_target="tpu_custom_call" | custom-call | tf_op jit(solution)/shard_map/pallas_call | solution.py:435
  3.0 7.3 %all-to-all-start = ((f32[32,2,1664]{2,1,0:T(2,128)}), f32[32,2,1664]{2,1,0:T(2,128)S(1)}, u32[]{:S(2)}, u32[]{:S(2)}) async-start(f32[32,2,1664]{2,1,0:T(2,128)} %shard_map.140.after_ref.after_hbm), calls=%async_computation | async-start | bytes 851968 | tf_op jit(solution)/shard_map/all_to_all | solution.py:480
  10.3 1.8 %shard_map.141 = (f32[128,1536]{1,0:T(8,128)S(1)}, f32[128,128]{1,0:T(8,128)S(1)}, f32[64,128]{1,0:T(8,128)S(1)}, bf16[192,128]{1,0:T(8,128)(2,1)S(1)}, bf16[192...) custom-call(s32[1]{0:T(128)} %bitcast.me_ref, ...), custom_call_target="tpu_custom_call" | custom-call | tf_op jit(solution)/shard_map/pallas_call | solution.py:435
  12.1 7.5 %shard_map.142 = (bf16[4608,1536]{1,0:T(8,128)(2,1)}, bf16[1024,1536]{1,0:T(8,128)(2,1)}, f32[8,128]{1,0:T(8,128)S(1)}) custom-call(s32[2,4608]{1,0:T(2,128)} %yielded_hbm.1, s32[2,4608]{1,0:T(2,128)} %consumed_hbm.3, f32[32,2,1664]{2,1,0:T(2,128)} %shard_map.140.after_ref.after_hbm), custom_call_target="tpu_custom_call" | custom-call | flops 283115520 | bytes 14155776 | tf_op jit(solution)/shard_map/pallas_call | solution.py:435
  19.6 4.4 %all-to-all-done.recv_ref = f32[32,2,1664]{2,1,0:T(2,128)S(1)} async-done(((f32[32,2,1664]{2,1,0:T(2,128)}), f32[32,2,1664]{2,1,0:T(2,128)S(1)}, u32[]{:S(2)}, u32[]{:S(2)}) %all-to-all-start) | async-done | bytes 426016 | tf_op jit(solution)/shard_map/all_to_all | solution.py:480
  24.0 0.5 shard_map.143
  24.6 0.1 collective-permute-start
  24.7 0.7 %collective-permute-start.1 = (f32[32,1536]{1,0:T(8,128)S(1)}, f32[32,1536]{1,0:T(8,128)S(1)}, u32[]{:S(2)}, u32[]{:S(2)}) collective-permute-start(f32[32,1536]{1,0:T(8,128)S(1)} %get-tuple-element.34), channel_id=1, source_target_pairs={{1,2},{2,1},{3,4},{4,3},{5,6},{6,5},{7,8},{8,7},{9,10},{10,9},{11,... | collective-permute-start | bytes 589832 | tf_op jit(solution)/shard_map/ppermute | solution.py:558
  25.3 6.1 %shard_map.144 = (bf16[1536,4608]{1,0:T(8,128)(2,1)S(1)}, bf16[4608,1536]{1,0:T(8,128)(2,1)S(1)}, bf16[4608,1536]{1,0:T(8,128)(2,1)S(1)}) custom-call(s32[2,4608]{1,0:T(2,128)S(1)} %get-tuple-element.35.consumed_ref, bf16[4608,1536]{1,0:T(8,128)(2,1)} %get-tuple-element.36.product_t_hbm, bf16[1024,1536]{1,0:T(8,128)(2,1)} %get-tuple-element.37.head_hbm, ...), custom_call_target="tpu_custom_call" | custom-call | flops 566231040 | bytes 28311552 | tf_op jit(solution)/shard_map/pallas_call | solution.py:435
  31.4 0.0 collective-permute-done.inner_ref
  31.4 0.0 collective-permute-done.1.outer_ref
  31.4 0.0 copy-start
  31.5 0.0 copy-start.1
  31.5 12.7 %shard_map.145 = (f32[128,1536]{1,0:T(8,128)}, f32[128,1536]{1,0:T(8,128)S(1)}, f32[32,2,1536]{2,1,0:T(2,128)}) custom-call(s32[1]{0:T(128)} %bitcast.me_ref, f32[128,1536]{1,0:T(8,128)S(1)} %get-tuple-element.31.flow_ref, f32[128,128]{1,0:T(8,128)S(1)} %get-tuple-element.32.after_ref.heat_ref, f32[32,1536]{1,0:T(8,128)S(1)} %collective-permute-done.inner_ref, ...), custom_call_target="tpu_custom_call" | custom-call | tf_op jit(solution)/shard_map/pallas_call | solution.py:435
  44.2 4.8 %all-to-all-start.1 = ((f32[32,2,1536]{2,1,0:T(2,128)}), f32[32,2,1536]{2,1,0:T(2,128)S(1)}, u32[]{:S(2)}, u32[]{:S(2)}) async-start(f32[32,2,1536]{2,1,0:T(2,128)} %get-tuple-element.49), calls=%async_computation.1 | async-start | bytes 786432 | tf_op jit(solution)/shard_map/all_to_all | solution.py:480
  49.1 0.0 copy-done
  49.1 0.0 copy-done.1
  49.1 0.4 shard_map.146
  49.5 12.8 %all-to-all-done.1.recv_ref = f32[32,2,1536]{2,1,0:T(2,128)S(1)} async-done(((f32[32,2,1536]{2,1,0:T(2,128)}), f32[32,2,1536]{2,1,0:T(2,128)S(1)}, u32[]{:S(2)}, u32[]{:S(2)}) %all-to-all-start.1) | async-done | bytes 393248 | tf_op jit(solution)/shard_map/all_to_all | solution.py:480
  62.2 1.2 %shard_map.147 = f32[128,1536]{1,0:T(8,128)} custom-call(f32[32,2,1536]{2,1,0:T(2,128)S(1)} %all-to-all-done.1.recv_ref, f32[128,64]{1,0:T(8,128)S(1)} %get-tuple-element.52.land_ref, f32[128,1536]{1,0:T(8,128)S(1)} %get-tuple-element.53.stay_ref), custom_call_target="tpu_custom_call" | custom-call | tf_op jit(solution)/shard_map/pallas_call | solution.py:435
Async XLA Ops:
  3.0 21.1 %all-to-all-start = ((f32[32,2,1664]{2,1,0:T(2,128)}), f32[32,2,1664]{2,1,0:T(2,128)S(1)}, u32[]{:S(2)}, u32[]{:S(2)}) async-start(f32[32,2,1664]{2,1,0:T(2,128)} %shard_map.140.after_ref.after_hbm), calls=%async_computation | async-start | bytes 851968 | tf_op jit(solution)/shard_map/all_to_all | solution.py:480
  24.6 6.9 %collective-permute-start = (f32[32,1536]{1,0:T(8,128)S(1)}, f32[32,1536]{1,0:T(8,128)S(1)}, u32[]{:S(2)}, u32[]{:S(2)}) collective-permute-start(f32[32,1536]{1,0:T(8,128)S(1)} %get-tuple-element.33), channel_id=1, source_target_pairs={{0,1},{1,0},{2,3},{3,2},{4,5},{5,4},{6,7},{7,6},{8,9},{9,8},{10,11... | collective-permute-start | bytes 589832 | tf_op jit(solution)/shard_map/ppermute | solution.py:557
  24.7 6.8 %collective-permute-start.1 = (f32[32,1536]{1,0:T(8,128)S(1)}, f32[32,1536]{1,0:T(8,128)S(1)}, u32[]{:S(2)}, u32[]{:S(2)}) collective-permute-start(f32[32,1536]{1,0:T(8,128)S(1)} %get-tuple-element.34), channel_id=1, source_target_pairs={{1,2},{2,1},{3,4},{4,3},{5,6},{6,5},{7,8},{8,7},{9,10},{10,9},{11,... | collective-permute-start | bytes 589832 | tf_op jit(solution)/shard_map/ppermute | solution.py:558
  31.4 17.6 %copy-start = (s32[128]{0:T(128)S(1)}, s32[128]{0:T(128)}, u32[]{:S(2)}) copy-start(s32[128]{0:T(128)} %param.20) | copy-start | bytes 1540
  31.5 17.6 %copy-start.1 = (s32[128]{0:T(128)S(1)}, s32[128]{0:T(128)}, u32[]{:S(2)}) copy-start(s32[128]{0:T(128)} %param.21) | copy-start | bytes 1540
  44.2 18.0 %all-to-all-start.1 = ((f32[32,2,1536]{2,1,0:T(2,128)}), f32[32,2,1536]{2,1,0:T(2,128)S(1)}, u32[]{:S(2)}, u32[]{:S(2)}) async-start(f32[32,2,1536]{2,1,0:T(2,128)} %get-tuple-element.49), calls=%async_computation.1 | async-start | bytes 786432 | tf_op jit(solution)/shard_map/all_to_all | solution.py:480
